TPU v7x, 32 devices: a whole 2x2x4 slice. The times are simulated.
32 devices in a mesh: groups: 2 (over x), branch: 4 (over y, core), head: 4 (over z).
Axes of the slice: x: 2, y: 2, z: 4, core: 2. Of those that a mesh axis runs over, the one named last changes fastest.
Arguments:
- queries: bfloat16 [128, 8192], P(('groups', 'branch'), 'head'), parts along dimension 0, may hold values from -100 to 100, as said below
- root_keys: bfloat16 [32768, 1024], P(('groups', 'branch'), 'head'), parts along dimension 0, may hold values from -6 to 6
- root_values: bfloat16 [32768, 1024], P(('groups', 'branch'), 'head'), parts along dimension 0, may hold values from -6 to 6
- branch_keys: bfloat16 [8, 4096, 1024], P(('groups', 'branch'), None, 'head'), parts along dimension 0, may hold values from -6 to 6
- branch_values: bfloat16 [8, 4096, 1024], P(('groups', 'branch'), None, 'head'), parts along dimension 0, may hold values from -6 to 6
- branch_lengths: int32 [8], P(('groups', 'branch')), parts along dimension 0, may hold values from 512 to 4096, as said below
- row_branch: int32 [128], P('groups'), parts along dimension 0, may hold values from 0 to 3, as said below
Outputs:
- attended: bfloat16 [128, 8192], P(('groups', 'branch'), 'head'), parts along dimension 0
There are 2 independent parts, one for each index of `groups`. A program takes and returns all parts, laid end to end along the dimension named above; each array names one. Nothing has to cross between parts.
Inputs may be any that keep to these rules, and one draw needn't show every extreme that they name: `queries`: query entries; rows may differ in scale. `row_branch`: no branch has more than 32 rows; some branch has exactly 32. `branch_lengths`: some branch has exactly 4096 live tokens.
All inputs are finite; a program needn't handle non-finite values.
Results may differ from a plain program's by a relative error of at most 0.006.
Values may be sent and summed in bfloat16 or wider, within the bound.
No kernel may reach another device: no remote copies, remote signals or barrier semaphores. Data moves between devices by JAX's collectives and lax.ppermute only.
A program may use at most 128 MiB of HBM per device.

v0:
```python
import jax
import jax.numpy as jnp
from jax import lax
from jax.sharding import PartitionSpec as P

QHEADS = 64
KVHEADS = 8
HD = 128


NEG = -1e30


def combined_all(value, axis, join):
    pieces = jax.tree.map(lambda part: lax.all_gather(part, axis), value)
    head = jax.tree.map(lambda part: part[0], pieces)
    tail = jax.tree.map(lambda part: part[1:], pieces)
    running, _ = lax.scan(lambda running, piece: (join(running, piece), None), head, tail)
    return running


def empty_part(count, width, head_dim):
    return (
        jnp.full((count, width), NEG, jnp.float32),
        jnp.zeros((count, width), jnp.float32),
        jnp.zeros((count, width, head_dim), jnp.float32),
    )


def combine(first, second):
    peak = jnp.maximum(first[0], second[0])
    scale_a = jnp.exp(first[0] - peak)
    scale_b = jnp.exp(second[0] - peak)
    return (
        peak,
        first[1] * scale_a + second[1] * scale_b,
        first[2] * scale_a[..., None] + second[2] * scale_b[..., None],
    )


def attend_block(query, keys, values, valid, factor):
    count, groups, per_group, head_dim = query.shape
    scores = jnp.einsum("rgph,bgh->rgpb", query, keys, preferred_element_type=jnp.float32) * factor
    scores = jnp.where(valid, scores, NEG)
    peak = jnp.max(scores, axis=-1)
    weights = jnp.where(valid, jnp.exp(scores - peak[..., None]), 0.0)
    total = jnp.sum(weights, axis=-1)
    mixed = jnp.einsum(
        "rgpb,bgh->rgph", weights.astype(jnp.bfloat16), values, preferred_element_type=jnp.float32
    )
    width = groups * per_group
    return (
        peak.reshape(count, width),
        total.reshape(count, width),
        mixed.reshape(count, width, head_dim),
    )


def on_device(
    queries, root_keys, root_values, branch_keys, branch_values, branch_lengths, row_branch
):
    head_dim = HD
    per_group = QHEADS // KVHEADS
    local_rows = queries.shape[0]
    all_rows = row_branch.shape[0]
    groups = root_keys.shape[1] // head_dim
    width = groups * per_group
    slots_count = 2 * local_rows
    factor = head_dim ** (-0.5)
    branch_id = lax.axis_index("branch")
    member = row_branch == branch_id
    ranking = jnp.cumsum(member.astype(jnp.int32)) - 1
    picker = member[None, :] & (
        ranking[None, :] == jnp.arange(slots_count, dtype=jnp.int32)[:, None]
    )
    picker_half = picker.astype(jnp.bfloat16)
    root_block = min(512, root_keys.shape[0])
    root_k = root_keys.reshape(root_keys.shape[0] // root_block, root_block, groups, head_dim)
    root_v = root_values.reshape(root_values.shape[0] // root_block, root_block, groups, head_dim)
    all_valid = jnp.ones((root_block,), dtype=bool)
    piece = lax.all_gather(queries, "branch", axis=0, tiled=True)
    count = piece.shape[0]
    query = piece.reshape(count, groups, per_group, head_dim)

    def one_block(state, pair):
        return (combine(state, attend_block(query, pair[0], pair[1], all_valid, factor)), None)

    part, _ = lax.scan(one_block, empty_part(count, width, head_dim), (root_k, root_v))
    peak_all = part[0]
    total_all = part[1]
    mixed_all = part[2]
    chosen = jnp.dot(picker_half, piece, preferred_element_type=jnp.float32)
    root_peak, root_total, root_mixed, chosen = (peak_all, total_all, mixed_all, chosen)
    branch_query = chosen.astype(jnp.bfloat16).reshape(slots_count, groups, per_group, head_dim)
    length = branch_lengths[0]
    keys_here = branch_keys[0]
    values_here = branch_values[0]
    block = min(512, keys_here.shape[0])
    blocks_used = (length + block - 1) // block

    def branch_step(index, state):
        offset = index * block
        keys_block = lax.dynamic_slice_in_dim(keys_here, offset, block, 0).reshape(
            block, groups, head_dim
        )
        values_block = lax.dynamic_slice_in_dim(values_here, offset, block, 0).reshape(
            block, groups, head_dim
        )
        valid = offset + jnp.arange(block, dtype=jnp.int32) < length
        return combine(state, attend_block(branch_query, keys_block, values_block, valid, factor))

    branch_part = lax.fori_loop(
        0, blocks_used, branch_step, empty_part(slots_count, width, head_dim)
    )
    picker_full = picker.astype(jnp.float32)
    spread_peak = jnp.max(jnp.where(picker[:, :, None], branch_part[0][:, None, :], NEG), axis=0)
    spread_total = jnp.einsum(
        "sr,sk->rk", picker_full, branch_part[1], precision=lax.Precision.HIGHEST
    )
    spread_mixed = jnp.einsum(
        "sr,sk->rk",
        picker_full,
        branch_part[2].reshape(slots_count, width * head_dim),
        precision=lax.Precision.HIGHEST,
    )
    peak, total, mixed = combine(
        (root_peak, root_total, root_mixed),
        (spread_peak, spread_total, spread_mixed.reshape(all_rows, width, head_dim)),
    )
    merged = combined_all((peak, total, mixed), "branch", combine)
    first_row = branch_id * local_rows
    own_total = lax.dynamic_slice_in_dim(merged[1], first_row, local_rows, 0)
    own_mixed = lax.dynamic_slice_in_dim(merged[2], first_row, local_rows, 0)
    finished = own_mixed / own_total[..., None]
    return finished.reshape(local_rows, width * head_dim).astype(jnp.bfloat16)


def solution(mesh):
    placed = (
        P(("groups", "branch"), "head"),
        P(("groups", "branch"), "head"),
        P(("groups", "branch"), "head"),
        P(("groups", "branch"), None, "head"),
        P(("groups", "branch"), None, "head"),
        P(("groups", "branch")),
        P("groups"),
    )
    return jax.shard_map(
        on_device,
        mesh=mesh,
        in_specs=placed,
        out_specs=P(("groups", "branch"), "head"),
        check_vma=False,
    )
```

profile of v0, /device:TPU:0, one launch (start us, length us, event | category | flops | bytes accessed | tf_op | source)
XLA Modules:
  0.0 119.2 jit_solution(15412547363303058967)
XLA Ops:
  7.2 4.1 %reshape.151 = bf16[8,512,2,128]{3,2,1,0:T(2,128)(2,1)} reshape(bf16[4096,256]{1,0:T(8,128)(2,1)} %param.14) | data formatting | bytes 4194304 | tf_op jit(solution)/shard_map/reshape | solution.py:78
  11.4 7.2 %all_gather.21 = bf16[64,2048]{1,0:T(8,128)(2,1)S(1)} all-gather(bf16[16,2048]{1,0:T(8,128)(2,1)S(1)} %copy-done.1), channel_id=1, replica_groups=mesh['groups'=2,'branch'=4,'head'=4] {'branch'}, dimensions={0}, use_global_device_ids=true | all-gather | bytes 327680 | tf_op jit(solution)/shard_map/all_gather | solution.py:81
  19.2 2.1 %reshape.152 = bf16[8,512,2,128]{3,2,1,0:T(2,128)(2,1)} reshape(bf16[4096,256]{1,0:T(8,128)(2,1)S(1)} %copy-done) | data formatting | bytes 4194304 | tf_op jit(solution)/shard_map/reshape | solution.py:79
  21.3 28.7 %while.45 = (s32[]{:T(128)}, f32[64,16]{0,1:T(8,128)S(1)}, f32[64,16]{0,1:T(8,128)S(1)}, f32[64,16,128]{2,0,1:T(8,128)S(1)}, bf16[8,512,2,128]{3,2,1,0:T(2,128)(...) while((s32[]{:T(128)}, f32[64,16]{0,1:T(8,128)S(1)}, ...), condition=%wide.region_3.4_spmd.clone, body=%wide.region_0.3_spmd.clone.sunk | while | flops 273160192 | bytes 10281076 | solution.py:88
  21.3 1.4 %constant_dynamic-slice_fusion.11 = (bf16[1,512,2,128]{3,2,1,0:T(2,128)(2,1)S(1)}, bf16[1,512,2,128]{3,2,1,0:T(2,128)(2,1)S(1)}) fusion(bf16[8,512,2,128]{3,2,1,0:T(2,128)(2,1)} %get-tuple-element.526, s32[]{:T(128)S(6)} %copy.127, bf16[8,512,2,128]{3,2,1,0:T(2,128)(2,1)} %get-tuple-element.524), kind=kLoop, calls=%fused_computation.53.clone.1 | loop fusion | bytes 1048580 | tf_op jit(solution)/shard_map/while/body/jit(dynamic_index_in_dim)/dynamic_slice | solution.py:88
  23.2 0.6 fusion.83
  24.9 1.4 %constant_dynamic-slice_fusion.11 = (bf16[1,512,2,128]{3,2,1,0:T(2,128)(2,1)S(1)}, bf16[1,512,2,128]{3,2,1,0:T(2,128)(2,1)S(1)}) fusion(bf16[8,512,2,128]{3,2,1,0:T(2,128)(2,1)} %get-tuple-element.526, s32[]{:T(128)S(6)} %copy.127, bf16[8,512,2,128]{3,2,1,0:T(2,128)(2,1)} %get-tuple-element.524), kind=kLoop, calls=%fused_computation.53.clone.1 | loop fusion | bytes 1048580 | tf_op jit(solution)/shard_map/while/body/jit(dynamic_index_in_dim)/dynamic_slice | solution.py:88
  26.8 0.6 fusion.83
  28.5 1.4 %constant_dynamic-slice_fusion.11 = (bf16[1,512,2,128]{3,2,1,0:T(2,128)(2,1)S(1)}, bf16[1,512,2,128]{3,2,1,0:T(2,128)(2,1)S(1)}) fusion(bf16[8,512,2,128]{3,2,1,0:T(2,128)(2,1)} %get-tuple-element.526, s32[]{:T(128)S(6)} %copy.127, bf16[8,512,2,128]{3,2,1,0:T(2,128)(2,1)} %get-tuple-element.524), kind=kLoop, calls=%fused_computation.53.clone.1 | loop fusion | bytes 1048580 | tf_op jit(solution)/shard_map/while/body/jit(dynamic_index_in_dim)/dynamic_slice | solution.py:88
  30.4 0.6 fusion.83
  32.1 1.4 %constant_dynamic-slice_fusion.11 = (bf16[1,512,2,128]{3,2,1,0:T(2,128)(2,1)S(1)}, bf16[1,512,2,128]{3,2,1,0:T(2,128)(2,1)S(1)}) fusion(bf16[8,512,2,128]{3,2,1,0:T(2,128)(2,1)} %get-tuple-element.526, s32[]{:T(128)S(6)} %copy.127, bf16[8,512,2,128]{3,2,1,0:T(2,128)(2,1)} %get-tuple-element.524), kind=kLoop, calls=%fused_computation.53.clone.1 | loop fusion | bytes 1048580 | tf_op jit(solution)/shard_map/while/body/jit(dynamic_index_in_dim)/dynamic_slice | solution.py:88
  34.0 0.6 fusion.83
  35.7 1.4 %constant_dynamic-slice_fusion.11 = (bf16[1,512,2,128]{3,2,1,0:T(2,128)(2,1)S(1)}, bf16[1,512,2,128]{3,2,1,0:T(2,128)(2,1)S(1)}) fusion(bf16[8,512,2,128]{3,2,1,0:T(2,128)(2,1)} %get-tuple-element.526, s32[]{:T(128)S(6)} %copy.127, bf16[8,512,2,128]{3,2,1,0:T(2,128)(2,1)} %get-tuple-element.524), kind=kLoop, calls=%fused_computation.53.clone.1 | loop fusion | bytes 1048580 | tf_op jit(solution)/shard_map/while/body/jit(dynamic_index_in_dim)/dynamic_slice | solution.py:88
  37.6 0.6 fusion.83
  39.2 1.4 %constant_dynamic-slice_fusion.11 = (bf16[1,512,2,128]{3,2,1,0:T(2,128)(2,1)S(1)}, bf16[1,512,2,128]{3,2,1,0:T(2,128)(2,1)S(1)}) fusion(bf16[8,512,2,128]{3,2,1,0:T(2,128)(2,1)} %get-tuple-element.526, s32[]{:T(128)S(6)} %copy.127, bf16[8,512,2,128]{3,2,1,0:T(2,128)(2,1)} %get-tuple-element.524), kind=kLoop, calls=%fused_computation.53.clone.1 | loop fusion | bytes 1048580 | tf_op jit(solution)/shard_map/while/body/jit(dynamic_index_in_dim)/dynamic_slice | solution.py:88
  41.2 0.6 fusion.83
  42.8 1.4 %constant_dynamic-slice_fusion.11 = (bf16[1,512,2,128]{3,2,1,0:T(2,128)(2,1)S(1)}, bf16[1,512,2,128]{3,2,1,0:T(2,128)(2,1)S(1)}) fusion(bf16[8,512,2,128]{3,2,1,0:T(2,128)(2,1)} %get-tuple-element.526, s32[]{:T(128)S(6)} %copy.127, bf16[8,512,2,128]{3,2,1,0:T(2,128)(2,1)} %get-tuple-element.524), kind=kLoop, calls=%fused_computation.53.clone.1 | loop fusion | bytes 1048580 | tf_op jit(solution)/shard_map/while/body/jit(dynamic_index_in_dim)/dynamic_slice | solution.py:88
  44.8 0.6 fusion.83
  46.4 1.4 %constant_dynamic-slice_fusion.11 = (bf16[1,512,2,128]{3,2,1,0:T(2,128)(2,1)S(1)}, bf16[1,512,2,128]{3,2,1,0:T(2,128)(2,1)S(1)}) fusion(bf16[8,512,2,128]{3,2,1,0:T(2,128)(2,1)} %get-tuple-element.526, s32[]{:T(128)S(6)} %copy.127, bf16[8,512,2,128]{3,2,1,0:T(2,128)(2,1)} %get-tuple-element.524), kind=kLoop, calls=%fused_computation.53.clone.1 | loop fusion | bytes 1048580 | tf_op jit(solution)/shard_map/while/body/jit(dynamic_index_in_dim)/dynamic_slice | solution.py:88
  48.4 0.6 fusion.83
  50.0 2.9 %copy.64 = bf16[1,4096,256]{1,2,0:T(8,128)(2,1)S(1)} copy(bf16[1,4096,256]{2,1,0:T(8,128)(2,1)} %param.16) | data formatting | bytes 4194304 | tf_op args[3]
  53.0 4.1 %copy.65 = bf16[1,4096,256]{1,2,0:T(8,128)(2,1)} copy(bf16[1,4096,256]{2,1,0:T(8,128)(2,1)} %param.17) | data formatting | bytes 4194304 | tf_op args[4]
  57.2 24.6 %while.43 = (s32[]{:T(128)}, f32[32,16]{0,1:T(8,128)S(1)}, f32[32,16]{0,1:T(8,128)S(1)}, f32[32,16,128]{2,0,1:T(8,128)S(1)}, s32[]{:T(128)}, /*index=5*/s32[]{:T...) while((s32[]{:T(128)}, f32[32,16]{0,1:T(8,128)S(1)}, ...), condition=%wide.region_8.9_spmd, body=%wide.region_5.8_spmd.sunk | while | flops 136776704 | bytes 5929151 | solution.py:112
  57.2 1.0 constant_dynamic-slice_fusion.9
  58.2 0.7 add_compare_fusion.2
  60.3 1.0 constant_dynamic-slice_fusion.9
  61.3 0.7 add_compare_fusion.2
  63.4 1.0 constant_dynamic-slice_fusion.9
  64.4 0.7 add_compare_fusion.2
  66.4 1.0 constant_dynamic-slice_fusion.9
  67.5 0.7 add_compare_fusion.2
  69.5 1.0 constant_dynamic-slice_fusion.9
  70.5 0.7 add_compare_fusion.2
  72.6 1.0 constant_dynamic-slice_fusion.9
  73.6 0.7 add_compare_fusion.2
  75.7 1.0 constant_dynamic-slice_fusion.9
  76.7 0.7 add_compare_fusion.2
  78.8 1.0 constant_dynamic-slice_fusion.9
  79.8 0.7 add_compare_fusion.2
  82.1 1.3 %fusion.29 = f32[64,16,128]{2,0,1:T(8,128)} fusion(f32[64,16,128]{2,0,1:T(8,128)S(1)} %get-tuple-element.136, f32[64,16]{0,1:T(8,128)S(1)} %get-tuple-element.318, f32[64,16]{0,1:T(8,128)S(1)} %get-tuple-element.317, s32[64]{0:T(128)S(1)} %add_reduce_fusion, pred[64]{0:T(512)(128)(4,1)S(1)} %get-tuple-element.308, f32[32,16,128]{2,0,1:T(8,128)S(1)} %get-tuple-element.137), kind=kOutput, calls=%fused_computation.58 | convolution fusion | flops 50728960 | bytes 1319232 | tf_op jit(solution)/shard_map/sr,sk->rk/dot_general | solution.py:120
  83.3 5.2 %all-gather.3 = f32[4,64,16]{1,2,0:T(8,128)S(1)} all-gather(f32[1,64,16]{1,2,0:T(8,128)S(1)} %get-tuple-element.319), channel_id=2, replica_groups=mesh['groups'=2,'branch'=4,'head'=4] {'branch'}, dimensions={0}, use_global_device_ids=true | all-gather | bytes 20480 | tf_op jit(solution)/shard_map/all_gather | solution.py:15
  88.7 5.2 %all-gather.4 = f32[4,64,16]{1,2,0:T(8,128)S(1)} all-gather(f32[1,64,16]{1,2,0:T(8,128)S(1)} %fusion.32), channel_id=3, replica_groups=mesh['groups'=2,'branch'=4,'head'=4] {'branch'}, dimensions={0}, use_global_device_ids=true | all-gather | bytes 20480 | tf_op jit(solution)/shard_map/all_gather | solution.py:15
  93.9 12.6 %all-gather.7.cloned.1.call-done = f32[256,16,128]{2,0,1:T(8,128)} async-done(((f32[64,16,128]{2,0,1:T(8,128)}), f32[256,16,128]{2,0,1:T(8,128)}) %all-gather.7.cloned.1.call-update) | async-done | bytes 2097168 | tf_op jit(solution)/shard_map/all_gather | solution.py:15
  106.4 1.1 slice.36
  107.8 1.1 slice-done
  108.9 2.5 %while.44 = (s32[]{:T(128)}, f32[64,16]{0,1:T(8,128)S(1)}, f32[64,16]{0,1:T(8,128)S(1)}, f32[64,16,128]{2,1,0:T(8,128)S(1)}, f32[3,64,16]{1,2,0:T(8,128)S(1)}, /...) while((s32[]{:T(128)}, f32[64,16]{0,1:T(8,128)S(1)}, f32[64,16]{0,1:T(8,128)S(1)}, ...), condition=%wide.region_11.12_spmd, body=%wide.region_10.11_spmd.sunk | while | flops 399362 | bytes 2678885 | solution.py:18
  110.8 0.6 fusion.80
  111.7 0.6 copy.112
  (123 shorter events, 26.9 us)
Async XLA Ops:
  6.5 99.9 %all-gather.7.cloned.1.call-start = ((), (), s32[]{:S(2)}) async-start(), calls=%async_computation | async-start | bytes 2621440 | tf_op jit(solution)/shard_map/all_gather | solution.py:15
  7.2 4.2 %copy-start.1 = (bf16[16,2048]{1,0:T(8,128)(2,1)S(1)}, bf16[16,2048]{1,0:T(8,128)(2,1)}, u32[]{:S(2)}) copy-start(bf16[16,2048]{1,0:T(8,128)(2,1)} %param.13) | copy-start | bytes 196612
  7.2 11.4 %copy-start.2 = (s32[64]{0:T(128)S(1)}, s32[64]{0:T(128)}, u32[]{:S(2)}) copy-start(s32[64]{0:T(128)} %param.19) | copy-start | bytes 772
  7.2 12.0 %copy-start = (bf16[4096,256]{1,0:T(8,128)(2,1)S(1)}, bf16[4096,256]{1,0:T(8,128)(2,1)}, u32[]{:S(2)}) copy-start(bf16[4096,256]{1,0:T(8,128)(2,1)} %param.15) | copy-start | bytes 6291460
  107.5 1.4 %slice-start = ((f32[256,16,128]{2,0,1:T(8,128)}), f32[192,16,128]{2,0,1:T(8,128)S(1)}, s32[]{:S(2)}) async-start(f32[256,16,128]{2,0,1:T(8,128)} %all-gather.7.cloned.1.call-done), calls=%async_computation.1 | async-start | bytes 3145728 | tf_op jit(solution)/shard_map/slice | solution.py:17
Sparse Core Ops, SparseCore 0:
  83.5 22.9 all-gather.6
where the time goes:
time: 121 us; the launch traced here: 119 us
  local copies, waits for them, and re-layouts  36.7 us (30%)
  other arithmetic  21.3 us (18%)
  blocking collectives  17.6 us (15%)
  matrix products  15.9 us (13%)
  between operations  14.2 us (12%)
  waiting for transfers between devices  12.6 us (10%)
    all_gather x1, waiting for transfers between devices, combined_all(): pieces = jax.tree.map(lambda part: lax.all_gather(part, axis), value)  12.6 us
    dynamic_slice x8, local copies, waits for them, and re-layouts, on_device(): lax.scan(one_block, empty_part(count, width, head_dim), (root_k, root_v))  11.2 us
    all_gather x2, blocking collectives, combined_all(): pieces = jax.tree.map(lambda part: lax.all_gather(part, axis), value)  10.4 us
    add x19, other arithmetic, combine(): first[2] * scale_a[..., None] + second[2] * scale_b[..., None]  8.01 us
    dynamic_slice x8, local copies, waits for them, and re-layouts, branch_step(): lax.dynamic_slice_in_dim(values_here, offset, block, 0)  7.99 us
    unnamed x12, local copies, waits for them, and re-layouts  7.84 us
    reduce_sum x16, other arithmetic, attend_block(): total = jnp.sum(weights, axis=-1)  7.32 us
    dot_general x16, matrix products, attend_block(): jnp.einsum('rgpb,bgh->rgph', weights.astype(jnp.bfloat16), values, prefer...  7.25 us
  transfers between devices with their start and end apart: 1, of which 1 were waited for; matrix products, arithmetic and copies ran while one was open for 0% of the time, Pallas kernels for 0%

commit v1 on v0

v1 whole, which is shorter than its diff:
```python
import functools

import jax
import jax.numpy as jnp
from jax import lax
from jax.experimental import pallas as pl
from jax.experimental.pallas import tpu as pltpu
from jax.sharding import PartitionSpec as P

QHEADS = 64
KVHEADS = 8
HD = 128
PER = QHEADS // KVHEADS
SCALE = HD**-0.5 * 1.4426950408889634
FEW = 16
LIMIT = 1e30
NEG = -1e30
F32 = jnp.float32
BF16 = jnp.bfloat16


def dot_nt(a, b):
    return lax.dot_general(a, b, (((1,), (1,)), ((), ())), preferred_element_type=F32)


def dot_nn(a, b):
    return lax.dot_general(a, b, (((1,), (0,)), ((), ())), preferred_element_type=F32)


def dot_tn(a, b):
    return lax.dot_general(a, b, (((0,), (0,)), ((), ())), preferred_element_type=F32)


def split3(x):
    high = x.astype(BF16)
    rest = x - high.astype(F32)
    mid = rest.astype(BF16)
    return high, mid, (rest - mid.astype(F32)).astype(BF16)


def stacked(query, group):
    return jnp.concatenate(
        [query[:, (group * PER + h) * HD : (group * PER + h + 1) * HD] for h in range(PER)], 0
    )


def add_block(query, mark, keys, values, live, acc):
    block = keys.shape[0]
    scores = dot_nt(keys, query)
    weights = jnp.exp2(scores * SCALE - mark * SCALE).astype(BF16)
    ones = jnp.ones((FEW, block), BF16)
    turned = values.T
    if live is not None:
        at = lax.broadcasted_iota(jnp.int32, (FEW, block), 1)
        ones = jnp.where(at < live, ones, jnp.zeros_like(ones))
        at = lax.broadcasted_iota(jnp.int32, (HD, block), 1)
        turned = jnp.where(at < live, turned, jnp.zeros_like(turned))
    acc[...] += dot_nn(jnp.concatenate([turned, ones], 0), weights)


def exact(query, keys_ref, values_ref, columns, length, acc, mark_ref):
    block = min(256, keys_ref.shape[0])
    mark_ref[...] = jnp.full(mark_ref.shape, NEG, F32)
    acc[...] = jnp.zeros(acc.shape, F32)

    @pl.loop(0, (length + block - 1) // block)
    def _(i):
        rows = pl.ds(pl.multiple_of(i * block, block), block)
        scores = dot_nt(keys_ref[rows, columns], query)
        valid = i * block + lax.broadcasted_iota(jnp.int32, scores.shape, 0) < length
        scores = jnp.where(valid, scores, NEG)
        old = mark_ref[...]
        new = jnp.maximum(old, jnp.max(scores, 0, keepdims=True))
        weights = jnp.where(valid, jnp.exp2((scores - new) * SCALE), 0.0)
        total = jnp.sum(weights, 0, keepdims=True)
        mixed = dot_tn(values_ref[rows, columns], weights.astype(BF16))
        more = jnp.concatenate([mixed, jnp.broadcast_to(total, (FEW, total.shape[1]))], 0)
        acc[...] = acc[...] * jnp.exp2((old - new) * SCALE) + more
        mark_ref[...] = new


def heads_last(rows, count):
    lines = [r[:, h * count : (h + 1) * count] for r in rows for h in range(PER)]
    lines.append(jnp.full((HD - len(lines), count), NEG, F32))
    return jnp.concatenate(lines, 0).T


def attend(
    pieces, axis, length_ref, owner_ref, *refs
):
    queries = refs[:pieces]
    root_k, root_v, branch_k, branch_v = refs[pieces : pieces + 4]
    outs = refs[pieces + 4 : 2 * pieces + 4]
    q_all, root_acc, root_mark, branch_acc, branch_mark = refs[2 * pieces + 4 :]
    local = queries[0].shape[0]
    rows = pieces * local
    slots = 2 * local
    width = queries[0].shape[1]
    groups = root_k.shape[1] // HD
    heads = groups * PER
    me = lax.axis_index(axis)
    length = length_ref[0]
    tokens = root_k.shape[0]

    for k in range(pieces):
        q_all[k * local : (k + 1) * local, :] = queries[k][...]

    row = lax.broadcasted_iota(jnp.int32, (rows, rows), 0)
    column = lax.broadcasted_iota(jnp.int32, (rows, rows), 1)
    moved = source_of(me, column // local, pieces) * local + lax.rem(column, local) == row
    owner = owner_ref[...].reshape(1, rows).astype(F32)
    owner = dot_nn(jnp.broadcast_to(owner, (8, rows)).astype(BF16), moved.astype(F32).astype(BF16))
    member = owner[:1] == me.astype(F32)
    before = dot_nn(
        jnp.broadcast_to(member.astype(F32), (8, rows)).astype(BF16),
        (row < column).astype(F32).astype(BF16),
    )[:1]
    slot = lax.broadcasted_iota(jnp.int32, (slots, rows), 0).astype(F32)
    picker = jnp.where(member & (before == slot), 1.0, 0.0).astype(BF16)
    chosen = dot_nn(picker, q_all[...]).astype(BF16)

    chunk = min(4 * local, rows)
    chunks = rows // chunk
    block = min(2048, tokens)

    def root(c, g):
        columns = slice(g * HD, (g + 1) * HD)
        query = stacked(q_all[pl.ds(pl.multiple_of(c * chunk, chunk), chunk), :], g)
        acc = root_acc.at[c, g]
        mark = jnp.max(dot_nt(root_k[:FEW, columns], query), 0, keepdims=True)
        root_mark[c, g] = mark
        acc[...] = jnp.zeros(acc.shape, F32)
        for i in range(tokens // block):
            part = slice(i * block, (i + 1) * block)
            add_block(query, mark, root_k[part, columns], root_v[part, columns], None, acc)

        @pl.when(jnp.logical_not(jnp.max(acc[HD : HD + 1, :]) < LIMIT))
        def _():
            exact(query, root_k, root_v, columns, tokens, acc, root_mark.at[c, g])

    def branch(g):
        columns = slice(g * HD, (g + 1) * HD)
        query = stacked(chosen, g)
        acc = branch_acc.at[g]
        mark = jnp.max(dot_nt(branch_k[:FEW, columns], query), 0, keepdims=True)
        branch_mark[g] = mark
        acc[...] = jnp.zeros(acc.shape, F32)
        size = min(1024, branch_k.shape[0])
        for i in range(branch_k.shape[0] // size):

            @pl.when(length > i * size)
            def _():
                part = slice(i * size, (i + 1) * size)
                add_block(
                    query, mark, branch_k[part, columns], branch_v[part, columns], length - i * size, acc
                )

        @pl.when(jnp.logical_not(jnp.max(acc[HD : HD + 1, :]) < LIMIT))
        def _():
            exact(query, branch_k, branch_v, columns, length, acc, branch_mark.at[g])

    if chunks == 1:
        for g in range(groups):
            root(0, g)
    else:

        @pl.loop(0, chunks)
        def _(c):
            for g in range(groups):
                root(c, g)

    for g in range(groups):
        branch(g)

    mixed_b = []
    for g in range(groups):
        turned = (branch_acc[g, :HD, :] / branch_acc[g, HD : HD + 1, :]).T
        mixed_b += [turned[h * slots : (h + 1) * slots] for h in range(PER)]
    mixed_b = jnp.concatenate(mixed_b, 1)
    level_b = heads_last(
        [branch_mark[g] * SCALE + jnp.log2(branch_acc[g, HD : HD + 1, :]) for g in range(groups)], slots
    )
    for c in range(chunks):
        there = slice(c * chunk, (c + 1) * chunk)
        pick = picker[:, there]
        high = mixed_b.astype(BF16)
        low = (mixed_b - high.astype(F32)).astype(BF16)
        spread = dot_tn(pick, high) + dot_tn(pick, low)
        first, second, third = split3(level_b)
        level = dot_tn(pick, first) + dot_tn(pick, second) + dot_tn(pick, third)
        held = jnp.sum(dot_tn(pick, jnp.ones((slots, HD), BF16)), 1, keepdims=True) > 0
        level = jnp.where(held, level, NEG)
        level_r = heads_last(
            [
                root_mark[c, g] * SCALE + jnp.log2(root_acc[c, g, HD : HD + 1, :])
                for g in range(groups)
            ],
            chunk,
        )
        top = jnp.maximum(level, level_r)
        weight_r = jnp.exp2(level_r - top)
        weight_b = jnp.exp2(level - top)
        total = weight_r + weight_b
        share_r = weight_r / total
        share_b = weight_b / total
        first, second, third = split3(top + jnp.log2(total))
        lanes = HD // 4
        aux = jnp.concatenate(
            [first[:, :lanes], second[:, :lanes], third[:, :lanes], first[:, :lanes]], 1
        )
        per_out = chunk // local
        for g in range(groups):
            turned = (root_acc[c, g, :HD, :] / root_acc[c, g, HD : HD + 1, :]).T
            for h in range(PER):
                head = g * PER + h
                tile = slice(head * HD, (head + 1) * HD)
                joined = (
                    turned[h * chunk : (h + 1) * chunk] * share_r[:, head : head + 1]
                    + spread[:, tile] * share_b[:, head : head + 1]
                ).astype(BF16)
                for j in range(per_out):
                    outs[c * per_out + j][:, tile] = joined[j * local : (j + 1) * local]
        for j in range(per_out):
            outs[c * per_out + j][:, width:] = aux[j * local : (j + 1) * local]


def join(pieces, *refs):
    parts, out = refs[:pieces], refs[pieces]
    width = out.shape[1]
    lanes = HD // 4
    levels = []
    for part in parts:
        aux = part[:, width:].astype(F32)
        levels.append(
            aux[:, :lanes] + aux[:, lanes : 2 * lanes] + aux[:, 2 * lanes : 3 * lanes]
        )
    top = functools.reduce(jnp.maximum, levels)
    weights = [jnp.exp2(level - top) for level in levels]
    total = functools.reduce(jnp.add, weights)
    shares = [weight / total for weight in weights]
    for head in range(width // HD):
        tile = slice(head * HD, (head + 1) * HD)
        out[:, tile] = functools.reduce(
            jnp.add,
            [
                part[:, tile].astype(F32) * share[:, head : head + 1]
                for part, share in zip(parts, shares)
            ],
        ).astype(BF16)


def source_of(me, step, count):
    if count & (count - 1) == 0:
        return me ^ step
    return lax.rem(me + step, count)


def pairs(step, count):
    return [(int(source_of_int(i, step, count)), i) for i in range(count)]


def source_of_int(me, step, count):
    return me ^ step if count & (count - 1) == 0 else (me + step) % count


def on_device(
    axis, count, queries, root_keys, root_values, branch_keys, branch_values, branch_lengths, row_branch
):
    local, width = queries.shape
    groups = root_keys.shape[1] // HD
    rows = count * local
    chunk = min(4 * local, rows)
    got = [queries] + [lax.ppermute(queries, axis, pairs(k, count)) for k in range(1, count)]
    vmem = pl.BlockSpec(memory_space=pltpu.VMEM)
    smem = pl.BlockSpec(memory_space=pltpu.SMEM)
    parts = pl.pallas_call(
        functools.partial(attend, count, axis),
        out_shape=[jax.ShapeDtypeStruct((local, width + HD), BF16)] * count,
        in_specs=[smem] + [vmem] * (count + 5),
        out_specs=[vmem] * count,
        scratch_shapes=[
            pltpu.VMEM((rows, width), BF16),
            pltpu.VMEM((rows // chunk, groups, HD + FEW, PER * chunk), F32),
            pltpu.VMEM((rows // chunk, groups, 1, PER * chunk), F32),
            pltpu.VMEM((groups, HD + FEW, PER * 2 * local), F32),
            pltpu.VMEM((groups, 1, PER * 2 * local), F32),
        ],
        compiler_params=pltpu.CompilerParams(vmem_limit_bytes=56 * 2**20),
        name="attend",
    )(
        branch_lengths,
        row_branch,
        *got,
        root_keys,
        root_values,
        branch_keys.reshape(branch_keys.shape[1:]),
        branch_values.reshape(branch_values.shape[1:]),
    )
    back = [parts[0]] + [
        lax.ppermute(parts[k], axis, [(b, a) for a, b in pairs(k, count)]) for k in range(1, count)
    ]
    return pl.pallas_call(
        functools.partial(join, count),
        out_shape=jax.ShapeDtypeStruct((local, width), BF16),
        in_specs=[vmem] * count,
        out_specs=vmem,
        name="join",
    )(*back)


def solution(mesh):
    placed = (
        P(("groups", "branch"), "head"),
        P(("groups", "branch"), "head"),
        P(("groups", "branch"), "head"),
        P(("groups", "branch"), None, "head"),
        P(("groups", "branch"), None, "head"),
        P(("groups", "branch")),
        P("groups"),
    )
    return jax.shard_map(
        functools.partial(on_device, "branch", mesh.shape["branch"]),
        mesh=mesh,
        in_specs=placed,
        out_specs=P(("groups", "branch"), "head"),
        check_vma=False,
    )
```

time: 121 us -> 63 us (0.52); the launches traced: 119 us -> 62.5 us
  Pallas kernels: 0 us -> 47.9 us
  local copies, waits for them, and re-layouts: 36.7 us -> 1.26 us
  other arithmetic: 21.3 us -> 0 us
  blocking collectives: 17.6 us -> 0 us
  matrix products: 15.9 us -> 0 us
  between operations: 14.2 us -> 0.67 us
  starting transfers between devices: 0.01 us -> 5.21 us
  waiting for transfers between devices: 12.6 us -> 7.49 us
    pallas_call x0 -> x2, Pallas kernels: none -> 47.9 us  [the longest x1 46 us: on_device(): pl.pallas_call(functools.partial(attend, count, axis), out_shape=[jax.Sha...]
    dynamic_slice x21 -> x0, local copies, waits for them, and re-layouts: 19.4 us -> none  [the longest x8 11.2 us: on_device(): lax.scan(one_block, empty_part(count, width, head_dim), (root_k, root_v))]
    all_gather x3 -> x0, blocking collectives: 17.6 us -> none  [the longest x2 10.4 us: combined_all(): pieces = jax.tree.map(lambda part: lax.all_gather(part, axis), value)]
    dot_general x35 -> x0, matrix products: 15.9 us -> none  [the longest x16 7.25 us: attend_block(): jnp.einsum('rgpb,bgh->rgph', weights.astype(jnp.bfloat16), values, prefer...]
    all_gather x1 -> x0, waiting for transfers between devices: 12.6 us -> none  [combined_all(): pieces = jax.tree.map(lambda part: lax.all_gather(part, axis), value)]
    add x38 -> x0, other arithmetic: 8.3 us -> none  [the longest x19 8.01 us: combine(): first[2] * scale_a[..., None] + second[2] * scale_b[..., None]]
    ppermute x0 -> x6, waiting for transfers between devices: none -> 7.49 us  [the longest x3 4.31 us: on_device(): lax.ppermute(parts[k], axis, [(b, a) for a, b in pairs(k, count)])]
    reduce_sum x16 -> x0, other arithmetic: 7.32 us -> none  [attend_block(): total = jnp.sum(weights, axis=-1)]
  transfers between devices with their start and end apart: 1 -> 6, of which waited for: 1 -> 4; matrix products, arithmetic and copies ran while one was open for 0% -> 0% of each run, Pallas kernels for 0% -> 0%
where the time goes in v1:
time: 63 us; the launch traced here: 62.5 us
  Pallas kernels  47.9 us (76%)
  waiting for transfers between devices  7.49 us (12%)
  starting transfers between devices  5.21 us (8%)
  local copies, waits for them, and re-layouts  1.26 us (2%)
  between operations  0.67 us (1%)
    pallas_call x1, Pallas kernels, on_device(): pl.pallas_call(functools.partial(attend, count, axis), out_shape=[jax.Sha...  46 us
    ppermute x3, waiting for transfers between devices, on_device(): lax.ppermute(parts[k], axis, [(b, a) for a, b in pairs(k, count)])  4.31 us
    ppermute x3, waiting for transfers between devices, on_device(): lax.ppermute(queries, axis, pairs(k, count))  3.18 us
    ppermute x3, starting transfers between devices, on_device(): lax.ppermute(queries, axis, pairs(k, count))  3.08 us
    ppermute x3, starting transfers between devices, on_device(): lax.ppermute(parts[k], axis, [(b, a) for a, b in pairs(k, count)])  2.13 us
    pallas_call x1, Pallas kernels, on_device(): pl.pallas_call(functools.partial(join, count), out_shape=jax.ShapeDtypeSt...  1.94 us
    unnamed x12, local copies, waits for them, and re-layouts  1.26 us
  transfers between devices with their start and end apart: 6, of which 4 were waited for; matrix products, arithmetic and copies ran while one was open for 0% of the time, Pallas kernels for 0%

profile of v1, /device:TPU:0, one launch (start us, length us, event | category | flops | bytes accessed | tf_op | source)
XLA Modules:
  0.0 62.5 jit_solution(11010667420665346450)
XLA Ops:
  0.0 3.0 %collective-permute-start.1 = (bf16[16,2048]{1,0:T(8,128)(2,1)}, bf16[16,2048]{1,0:T(8,128)(2,1)S(1)}, u32[]{:S(2)}, u32[]{:S(2)}) collective-permute-start(bf16[16,2048]{1,0:T(8,128)(2,1)} %refs_0_.1), channel_id=1, source_target_pairs={{8,0},{12,4},{0,8},{4,12},{9,1},{13,5},{1,9},{5,13},{10,2},{14,6},... | collective-permute-start | bytes 196616 | tf_op jit(solution)/shard_map/ppermute | solution.py:273
  3.0 0.0 collective-permute-start
  3.0 0.1 collective-permute-start.2
  3.7 1.9 %collective-permute-done.1.refs_2_ = bf16[16,2048]{1,0:T(8,128)(2,1)S(1)} collective-permute-done((bf16[16,2048]{1,0:T(8,128)(2,1)}, bf16[16,2048]{1,0:T(8,128)(2,1)S(1)}, u32[]{:S(2)}, u32[]{:S(2)}) %collective-permute-start.1) | collective-permute-done | bytes 65568 | tf_op jit(solution)/shard_map/ppermute | solution.py:273
  5.6 0.0 copy-start.3
  5.6 0.0 collective-permute-done.refs_1_
  5.6 0.0 copy-start.4
  5.6 1.3 %collective-permute-done.2.refs_3_ = bf16[16,2048]{1,0:T(8,128)(2,1)S(1)} collective-permute-done((bf16[16,2048]{1,0:T(8,128)(2,1)}, bf16[16,2048]{1,0:T(8,128)(2,1)S(1)}, u32[]{:S(2)}, u32[]{:S(2)}) %collective-permute-start.2) | collective-permute-done | bytes 65568 | tf_op jit(solution)/shard_map/ppermute | solution.py:273
  6.9 0.0 copy-start.5
  6.9 0.0 copy-done.3
  6.9 0.0 copy-done.4
  6.9 0.6 copy-done.5
  7.6 46.0 %attend.1 = (bf16[16,2176]{1,0:T(8,128)(2,1)}, bf16[16,2176]{1,0:T(8,128)(2,1)}, bf16[16,2176]{1,0:T(8,128)(2,1)}, bf16[16,2176]{1,0:T(8,128)(2,1)}) custom-call(s32[1]{0:T(128)S(6)} %copy.8.length_ref, s32[64]{0:T(128)} %owner_ref.1, bf16[16,2048]{1,0:T(8,128)(2,1)} %refs_0_.1, bf16[16,2048]{1,0:T(8,128)(2,1)} %copy-done.4, bf16[16,2048]{1,0:T(8,128)(2,1)} %copy-done.3, ...), custom_call_target="tpu_custom_call" | custom-call | tf_op jit(solution)/shard_map/attend/pallas_call | solution.py:276
  53.5 0.0 collective-permute-start.3
  53.5 2.0 %collective-permute-start.4 = (bf16[16,2176]{1,0:T(8,128)(2,1)}, bf16[16,2176]{1,0:T(8,128)(2,1)S(1)}, u32[]{:S(2)}, u32[]{:S(2)}) collective-permute-start(bf16[16,2176]{1,0:T(8,128)(2,1)} %get-tuple-element.11), channel_id=1, source_target_pairs={{0,8},{4,12},{8,0},{12,4},{1,9},{5,13},{9,1},{13,5},{2,10},{6,14},... | collective-permute-start | bytes 208904 | tf_op jit(solution)/shard_map/ppermute | solution.py:300
  55.5 0.1 collective-permute-start.5
  55.6 0.0 collective-permute-done.3.refs_1_
  55.6 0.0 copy-start
  55.6 2.9 %collective-permute-done.4.refs_2_ = bf16[16,2176]{1,0:T(8,128)(2,1)S(1)} collective-permute-done((bf16[16,2176]{1,0:T(8,128)(2,1)}, bf16[16,2176]{1,0:T(8,128)(2,1)S(1)}, u32[]{:S(2)}, u32[]{:S(2)}) %collective-permute-start.4) | collective-permute-done | bytes 69664 | tf_op jit(solution)/shard_map/ppermute | solution.py:300
  58.6 0.0 copy-start.1
  58.6 1.4 %collective-permute-done.5.refs_3_ = bf16[16,2176]{1,0:T(8,128)(2,1)S(1)} collective-permute-done((bf16[16,2176]{1,0:T(8,128)(2,1)}, bf16[16,2176]{1,0:T(8,128)(2,1)S(1)}, u32[]{:S(2)}, u32[]{:S(2)}) %collective-permute-start.5) | collective-permute-done | bytes 69664 | tf_op jit(solution)/shard_map/ppermute | solution.py:300
  60.0 0.0 copy-start.2
  60.0 0.0 copy-done
  60.0 0.0 copy-done.1
  60.0 0.6 copy-done.2
  60.6 1.9 %join.1 = bf16[16,2048]{1,0:T(8,128)(2,1)} custom-call(bf16[16,2176]{1,0:T(8,128)(2,1)} %get-tuple-element.9.refs_0_, bf16[16,2176]{1,0:T(8,128)(2,1)} %copy-done, bf16[16,2176]{1,0:T(8,128)(2,1)} %copy-done.1, bf16[16,2176]{1,0:T(8,128)(2,1)} %copy-done.2), custom_call_target="tpu_custom_call" | custom-call | tf_op jit(solution)/shard_map/join/pallas_call | solution.py:302
Async XLA Ops:
  0.0 5.6 %collective-permute-start.1 = (bf16[16,2048]{1,0:T(8,128)(2,1)}, bf16[16,2048]{1,0:T(8,128)(2,1)S(1)}, u32[]{:S(2)}, u32[]{:S(2)}) collective-permute-start(bf16[16,2048]{1,0:T(8,128)(2,1)} %refs_0_.1), channel_id=1, source_target_pairs={{8,0},{12,4},{0,8},{4,12},{9,1},{13,5},{1,9},{5,13},{10,2},{14,6},... | collective-permute-start | bytes 196616 | tf_op jit(solution)/shard_map/ppermute | solution.py:273
  3.0 2.6 %collective-permute-start = (bf16[16,2048]{1,0:T(8,128)(2,1)}, bf16[16,2048]{1,0:T(8,128)(2,1)S(1)}, u32[]{:S(2)}, u32[]{:S(2)}) collective-permute-start(bf16[16,2048]{1,0:T(8,128)(2,1)} %refs_0_.1), channel_id=1, source_target_pairs={{4,0},{0,4},{12,8},{8,12},{5,1},{1,5},{13,9},{9,13},{6,2},{2,6},{1... | collective-permute-start | bytes 196616 | tf_op jit(solution)/shard_map/ppermute | solution.py:273
  3.0 4.0 %collective-permute-start.2 = (bf16[16,2048]{1,0:T(8,128)(2,1)}, bf16[16,2048]{1,0:T(8,128)(2,1)S(1)}, u32[]{:S(2)}, u32[]{:S(2)}) collective-permute-start(bf16[16,2048]{1,0:T(8,128)(2,1)} %refs_0_.1), channel_id=1, source_target_pairs={{12,0},{8,4},{4,8},{0,12},{13,1},{9,5},{5,9},{1,13},{14,2},{10,6},... | collective-permute-start | bytes 196616 | tf_op jit(solution)/shard_map/ppermute | solution.py:273
  5.6 1.3 %copy-start.3 = (bf16[16,2048]{1,0:T(8,128)(2,1)}, bf16[16,2048]{1,0:T(8,128)(2,1)S(1)}, u32[]{:S(2)}) copy-start(bf16[16,2048]{1,0:T(8,128)(2,1)S(1)} %collective-permute-done.1.refs_2_) | copy-start | bytes 196612
  5.6 1.3 %copy-start.4 = (bf16[16,2048]{1,0:T(8,128)(2,1)}, bf16[16,2048]{1,0:T(8,128)(2,1)S(1)}, u32[]{:S(2)}) copy-start(bf16[16,2048]{1,0:T(8,128)(2,1)S(1)} %collective-permute-done.refs_1_) | copy-start | bytes 196612
  6.9 0.6 %copy-start.5 = (bf16[16,2048]{1,0:T(8,128)(2,1)}, bf16[16,2048]{1,0:T(8,128)(2,1)S(1)}, u32[]{:S(2)}) copy-start(bf16[16,2048]{1,0:T(8,128)(2,1)S(1)} %collective-permute-done.2.refs_3_) | copy-start | bytes 196612
  53.5 2.1 %collective-permute-start.3 = (bf16[16,2176]{1,0:T(8,128)(2,1)}, bf16[16,2176]{1,0:T(8,128)(2,1)S(1)}, u32[]{:S(2)}, u32[]{:S(2)}) collective-permute-start(bf16[16,2176]{1,0:T(8,128)(2,1)} %get-tuple-element.10), channel_id=1, source_target_pairs={{0,4},{4,0},{8,12},{12,8},{1,5},{5,1},{9,13},{13,9},{2,6},{6,2},{1... | collective-permute-start | bytes 208904 | tf_op jit(solution)/shard_map/ppermute | solution.py:300
  53.5 5.0 %collective-permute-start.4 = (bf16[16,2176]{1,0:T(8,128)(2,1)}, bf16[16,2176]{1,0:T(8,128)(2,1)S(1)}, u32[]{:S(2)}, u32[]{:S(2)}) collective-permute-start(bf16[16,2176]{1,0:T(8,128)(2,1)} %get-tuple-element.11), channel_id=1, source_target_pairs={{0,8},{4,12},{8,0},{12,4},{1,9},{5,13},{9,1},{13,5},{2,10},{6,14},... | collective-permute-start | bytes 208904 | tf_op jit(solution)/shard_map/ppermute | solution.py:300
  55.5 4.4 %collective-permute-start.5 = (bf16[16,2176]{1,0:T(8,128)(2,1)}, bf16[16,2176]{1,0:T(8,128)(2,1)S(1)}, u32[]{:S(2)}, u32[]{:S(2)}) collective-permute-start(bf16[16,2176]{1,0:T(8,128)(2,1)} %get-tuple-element.12), channel_id=1, source_target_pairs={{0,12},{4,8},{8,4},{12,0},{1,13},{5,9},{9,5},{13,1},{2,14},{6,10},... | collective-permute-start | bytes 208904 | tf_op jit(solution)/shard_map/ppermute | solution.py:300
  55.6 4.3 %copy-start = (bf16[16,2176]{1,0:T(8,128)(2,1)}, bf16[16,2176]{1,0:T(8,128)(2,1)S(1)}, u32[]{:S(2)}) copy-start(bf16[16,2176]{1,0:T(8,128)(2,1)S(1)} %collective-permute-done.3.refs_1_) | copy-start | bytes 208900
  58.6 1.4 %copy-start.1 = (bf16[16,2176]{1,0:T(8,128)(2,1)}, bf16[16,2176]{1,0:T(8,128)(2,1)S(1)}, u32[]{:S(2)}) copy-start(bf16[16,2176]{1,0:T(8,128)(2,1)S(1)} %collective-permute-done.4.refs_2_) | copy-start | bytes 208900
  60.0 0.6 %copy-start.2 = (bf16[16,2176]{1,0:T(8,128)(2,1)}, bf16[16,2176]{1,0:T(8,128)(2,1)S(1)}, u32[]{:S(2)}) copy-start(bf16[16,2176]{1,0:T(8,128)(2,1)S(1)} %collective-permute-done.5.refs_3_) | copy-start | bytes 208900

commit v2 on v0

v2 whole, which is shorter than its diff:
```python
import functools

import jax
import jax.numpy as jnp
from jax import lax
from jax.experimental import pallas as pl
from jax.experimental.pallas import tpu as pltpu
from jax.sharding import PartitionSpec as P

QHEADS = 64
KVHEADS = 8
HD = 128
PER = QHEADS // KVHEADS
SCALE = HD**-0.5 * 1.4426950408889634
FEW = 16
LIMIT = 1e30
NEG = -1e30
LANES = HD // 4
BLOCK = 2048
F32 = jnp.float32
BF16 = jnp.bfloat16


def dot_nt(a, b):
    return lax.dot_general(a, b, (((1,), (1,)), ((), ())), preferred_element_type=F32)


def dot_nn(a, b):
    return lax.dot_general(a, b, (((1,), (0,)), ((), ())), preferred_element_type=F32)


def dot_tn(a, b):
    return lax.dot_general(a, b, (((0,), (0,)), ((), ())), preferred_element_type=F32)


def split3(x):
    high = x.astype(BF16)
    rest = x - high.astype(F32)
    mid = rest.astype(BF16)
    return high, mid, (rest - mid.astype(F32)).astype(BF16)


def source_of(me, step, count):
    if count & (count - 1) == 0:
        return me ^ step
    return (me + step) % count


def stacked(query, group):
    first = group * PER
    return jnp.concatenate([query[:, h * HD : (h + 1) * HD] for h in range(first, first + PER)], 0)


def turned_values(values, live):
    ones = jnp.ones((FEW, values.shape[0]), BF16)
    both = jnp.concatenate([values.T, ones], 0)
    if live is None:
        return both
    at = lax.broadcasted_iota(jnp.int32, both.shape, 1)
    return jnp.where(at < live, both, jnp.zeros_like(both))


def of_group(keys_ref, turned_ref, group, there):
    wide = keys_ref.shape[1]
    columns = slice(group * HD, (group + 1) * HD)
    turned = jnp.concatenate([turned_ref[columns, there], turned_ref[wide:, there]], 0)
    return keys_ref[there, columns], turned


def weighted(keys_ref, turned_ref, group, there, query, mark):
    keys, turned = of_group(keys_ref, turned_ref, group, there)
    weights = jnp.exp2(dot_nt(keys, query) * SCALE - mark * SCALE)
    return dot_nn(turned, weights.astype(BF16))


def blocks(tokens):
    size = min(BLOCK, tokens)
    return [slice(i, i + size) for i in range(0, tokens, size)]


def attend(query, keys_ref, turned_ref, acc, marks, length=None):
    groups = acc.shape[0]
    queries = [stacked(query, g) for g in range(groups)]
    whole = blocks(keys_ref.shape[0])
    first = whole[:1] if length is not None else whole
    for g, q in enumerate(queries):
        mark = jnp.max(dot_nt(keys_ref[:FEW, g * HD : (g + 1) * HD], q), 0, keepdims=True)
        marks[g] = mark
        parts = [weighted(keys_ref, turned_ref, g, there, q, mark) for there in first]
        acc[g] = functools.reduce(jnp.add, parts)
    for there in whole[len(first) :]:

        @pl.when(length > there.start)
        def _():
            for g, q in enumerate(queries):
                acc[g] += weighted(keys_ref, turned_ref, g, there, q, marks[g])


def overflowed(acc):
    return jnp.max(jnp.where(acc[:, HD : HD + 1, :] < LIMIT, 0.0, 1.0)) > 0.0


def again(query, keys_ref, turned_ref, acc, marks, length):
    block = min(256, keys_ref.shape[0])
    for g in range(acc.shape[0]):
        q = stacked(query, g)
        marks[g] = jnp.full(marks.shape[1:], NEG, F32)
        acc[g] = jnp.zeros(acc.shape[1:], F32)

        @pl.loop(0, (length + block - 1) // block)
        def _(i):
            keys, turned = of_group(
                keys_ref, turned_ref, g, pl.ds(pl.multiple_of(i * block, block), block)
            )
            scores = dot_nt(keys, q)
            valid = i * block + lax.broadcasted_iota(jnp.int32, scores.shape, 0) < length
            scores = jnp.where(valid, scores, NEG)
            old = marks[g]
            new = jnp.maximum(old, jnp.max(scores, 0, keepdims=True))
            weights = jnp.where(valid, jnp.exp2((scores - new) * SCALE), 0.0)
            acc[g] = acc[g] * jnp.exp2((old - new) * SCALE) + dot_nn(turned, weights.astype(BF16))
            marks[g] = new


def finish(acc, marks):
    groups = acc.shape[0]
    rows = acc.shape[2] // PER
    tiles, lines = [], []
    for g in range(groups):
        total = acc[g, HD : HD + 1, :]
        mean = (acc[g, :HD, :] * (1.0 / total)).T
        tiles += [mean[h * rows : (h + 1) * rows] for h in range(PER)]
        level = marks[g] * SCALE + jnp.log2(total)
        lines += [level[:, h * rows : (h + 1) * rows] for h in range(PER)]
    lines.append(jnp.full((HD - len(lines), rows), NEG, F32))
    return tiles, jnp.concatenate(lines, 0).T


def joined(tiles, level, spread, level_b):
    top = jnp.maximum(level, level_b)
    weight = jnp.exp2(level - top)
    weight_b = jnp.exp2(level_b - top)
    total = weight + weight_b
    share = weight / total
    share_b = weight_b / total
    tiles = [
        mean * share[:, head : head + 1]
        + spread[:, head * HD : (head + 1) * HD] * share_b[:, head : head + 1]
        for head, mean in enumerate(tiles)
    ]
    return tiles, top + jnp.log2(total)


def pack(tiles, level, out):
    for head, mean in enumerate(tiles):
        out[:, head * HD : (head + 1) * HD] = mean.astype(BF16)
    parts = [p[:, :LANES] for p in split3(level)]
    out[:, len(tiles) * HD :] = jnp.concatenate(parts + parts[:1], 1)


def prepare(
    count, axis, length_ref, owner_hbm, query_hbm, root_k_hbm, root_v_hbm, branch_k_hbm, branch_v_hbm,
    root_k, root_t, branch_k, branch_t, query_ref, picker_ref, owner_ref, root_v, branch_v, sems,
):
    local = query_ref.shape[0]
    rows = count * local
    slots = 2 * local
    copies = []

    def fetch(source, target):
        copies.append(pltpu.make_async_copy(source, target, sems.at[len(copies)]))
        return copies[-1]

    small = [fetch(owner_hbm, owner_ref), fetch(query_hbm, query_ref)]
    values = []
    for source, target, turned in ((root_v_hbm, root_v, root_t), (branch_v_hbm, branch_v, branch_t)):
        for there in parts_of(source.shape[0]):
            copy = fetch(source.at[pl.ds(there.start, there.stop - there.start), :], target.at[there, :])
            values.append((copy, target, turned, there))
    keys = [fetch(root_k_hbm, root_k), fetch(branch_k_hbm, branch_k)]
    for copy in copies:
        copy.start()

    me = lax.axis_index(axis)
    row = lax.broadcasted_iota(jnp.int32, (rows, rows), 0)
    column = lax.broadcasted_iota(jnp.int32, (rows, rows), 1)
    moved = source_of(me, column // local, count) * local + column % local == row
    small[0].wait()
    owner = owner_ref[...].reshape(1, rows).astype(F32)
    owner = dot_nn(jnp.broadcast_to(owner, (8, rows)).astype(BF16), moved.astype(F32).astype(BF16))
    member = owner[:1] == me.astype(F32)
    before = dot_nn(
        jnp.broadcast_to(member.astype(F32), (8, rows)).astype(BF16),
        (row < column).astype(F32).astype(BF16),
    )[:1]
    slot = lax.broadcasted_iota(jnp.int32, (slots, rows), 0).astype(F32)
    picker_ref[...] = jnp.where(member & (before == slot), 1.0, 0.0).astype(BF16)

    length = length_ref[0]
    for copy, source, turned, there in values:
        copy.wait()
        live = length - there.start if turned is branch_t else None
        turned[:, there] = turned_values(source[there, :], live)
    for copy in (small[1], *keys):
        copy.wait()


def parts_of(tokens):
    size = min(1024, tokens)
    return [slice(i, i + size) for i in range(0, tokens, size)]


def unit(first, second, root_k, root_t, mean_ref, level_ref, acc, marks):
    query = jnp.concatenate([first[...], second[...]], 0)
    attend(query, root_k, root_t, acc, marks)

    @pl.when(overflowed(acc))
    def _():
        again(query, root_k, root_t, acc, marks, root_k.shape[0])

    tiles, level = finish(acc, marks)
    for head, mean in enumerate(tiles):
        mean_ref[:, head * HD : (head + 1) * HD] = mean
    level_ref[...] = level


def main(count, *refs):
    length_ref, picker_ref, root_k, root_t, branch_k, branch_t = refs[:6]
    refs = refs[6:]
    queries, refs = refs[:count], refs[count:]
    more = max(0, count // 2 - 2)
    means, refs = refs[:more], refs[more:]
    levels, refs = refs[:more], refs[more:]
    outs, refs = refs[: count - 2], refs[count - 2 :]
    spread_ref, level_ref, root_acc, root_marks, branch_acc, branch_marks = refs
    local = queries[0].shape[0]
    length = length_ref[0]
    picker = picker_ref[...]
    pieces = [q[...] for q in queries]
    query = jnp.concatenate(pieces[2:4], 0)
    chosen = dot_nn(picker, jnp.concatenate(pieces, 0)).astype(BF16)
    attend(query, root_k, root_t, root_acc, root_marks)
    attend(chosen, branch_k, branch_t, branch_acc, branch_marks, length)

    @pl.when(overflowed(root_acc) | overflowed(branch_acc))
    def _():
        again(query, root_k, root_t, root_acc, root_marks, root_k.shape[0])
        again(chosen, branch_k, branch_t, branch_acc, branch_marks, length)

    tiles, level = finish(branch_acc, branch_marks)
    mixed = jnp.concatenate(tiles, 1)
    high = mixed.astype(BF16)
    low = (mixed - high.astype(F32)).astype(BF16)
    parts = split3(level)
    spread = dot_tn(picker, high) + dot_tn(picker, low)
    level_b = functools.reduce(jnp.add, [dot_tn(picker, part) for part in parts])
    held = dot_tn(picker, jnp.ones((2 * local, HD), BF16)) > 0.0
    level_b = jnp.where(held, level_b, NEG)
    spread_ref[...] = spread[: 2 * local]
    level_ref[...] = level_b[: 2 * local]
    for pair in range(1, count // 2):
        if pair == 1:
            tiles, level = finish(root_acc, root_marks)
        else:
            mean = means[pair - 2][...]
            tiles = [mean[:, i : i + HD] for i in range(0, mean.shape[1], HD)]
            level = levels[pair - 2][...]
        there = slice(2 * pair * local, 2 * (pair + 1) * local)
        tiles, level = joined(tiles, level, spread[there], level_b[there])
        for j in range(2):
            mine = slice(j * local, (j + 1) * local)
            pack([t[mine] for t in tiles], level[mine], outs[2 * (pair - 1) + j])


def local_pair(first, second, root_k, root_t, spread, level_b, mean_ref, level_ref, out, acc, marks):
    local = first.shape[0]
    query = jnp.concatenate([first[...], second[...]], 0)
    attend(query, root_k, root_t, acc, marks)

    @pl.when(overflowed(acc))
    def _():
        again(query, root_k, root_t, acc, marks, root_k.shape[0])

    tiles, level = finish(acc, marks)
    tiles, level = joined(tiles, level, spread[...], level_b[...])
    pack([t[local:] for t in tiles], level[local:], out)
    for head, mean in enumerate(tiles):
        mean_ref[:, head * HD : (head + 1) * HD] = mean[:local]
    level_ref[...] = level[:local]


def join(*refs):
    mean, level, out = refs[-3:]
    parts = refs[:-3]
    width = out.shape[1]
    levels = [level[:, :LANES]]
    for part in parts:
        aux = part[:, width:].astype(F32)
        levels.append(aux[:, :LANES] + aux[:, LANES : 2 * LANES] + aux[:, 2 * LANES : 3 * LANES])
    top = functools.reduce(jnp.maximum, levels)
    weights = [jnp.exp2(level - top) for level in levels]
    over = 1.0 / functools.reduce(jnp.add, weights)
    shares = [weight * over for weight in weights]
    for head in range(width // HD):
        tile = slice(head * HD, (head + 1) * HD)
        terms = [
            part[:, tile].astype(F32) * share[:, head : head + 1]
            for part, share in zip((mean, *parts), shares)
        ]
        out[:, tile] = functools.reduce(jnp.add, terms).astype(BF16)


def near(x):
    return pltpu.with_memory_space_constraint(x, pltpu.VMEM)


def call(kernel, name, outs, scratch, operands, smem=0, far=0, room=24, cost=None):
    vmem = pl.BlockSpec(memory_space=pltpu.VMEM)
    return pl.pallas_call(
        kernel,
        out_shape=[pltpu.VMEM(shape, dtype) for shape, dtype in outs],
        in_specs=[pl.BlockSpec(memory_space=pltpu.SMEM)] * smem
        + [pl.BlockSpec(memory_space=pltpu.HBM)] * far
        + [vmem] * (len(operands) - smem - far),
        out_specs=[vmem] * len(outs),
        scratch_shapes=scratch,
        compiler_params=pltpu.CompilerParams(vmem_limit_bytes=room * 2**20),
        cost_estimate=cost,
        name=name,
    )(
        *operands[:smem],
        *[pltpu.with_memory_space_constraint(x, pltpu.HBM) for x in operands[smem : smem + far]],
        *map(near, operands[smem + far :]),
    )


def on_device(
    axis, count, queries, root_keys, root_values, branch_keys, branch_values, branch_lengths, row_branch
):
    local, width = queries.shape
    tokens, wide = root_keys.shape
    kept = branch_keys.shape[1]
    pair = 2 * local
    columns = pair * PER
    sums = [
        pltpu.VMEM((wide // HD, HD + FEW, columns), F32),
        pltpu.VMEM((wide // HD, 1, columns), F32),
    ]
    message = ((local, width + HD), BF16)
    pair_form = [((pair, width), F32), ((pair, HD), F32)]

    def moved(x, step, back=False):
        pairs = [(source_of(i, step, count), i) for i in range(count)]
        return lax.ppermute(x, axis, [(b, a) for a, b in pairs] if back else pairs)

    got = {k: moved(queries, k) for k in [*range(2, count), 1]}
    root_k, root_t, branch_k, branch_t, own, picker = call(
        functools.partial(prepare, count, axis),
        "prepare",
        [
            ((tokens, wide), BF16),
            ((wide + FEW, tokens), BF16),
            ((kept, wide), BF16),
            ((wide + FEW, kept), BF16),
            ((local, width), BF16),
            ((pair, count * local), BF16),
        ],
        [
            pltpu.VMEM((count * local,), jnp.int32),
            pltpu.VMEM((tokens, wide), BF16),
            pltpu.VMEM((kept, wide), BF16),
            pltpu.SemaphoreType.DMA((4 + len(parts_of(tokens)) + len(parts_of(kept)),)),
        ],
        [
            branch_lengths,
            row_branch,
            queries,
            root_keys,
            root_values,
            branch_keys.reshape(branch_keys.shape[1:]),
            branch_values.reshape(branch_values.shape[1:]),
        ],
        smem=1,
        far=6,
    )
    got[0] = own
    units = [
        call(unit, "unit", pair_form, sums, [got[k], got[k + 1], root_k, root_t])
        for k in range(4, count, 2)
    ]
    *outs, spread, level_b = call(
        functools.partial(main, count),
        "main",
        [message] * (count - 2) + pair_form,
        sums + sums,
        [branch_lengths, picker, root_k, root_t, branch_k, branch_t]
        + [got[k] for k in range(count)]
        + [u[0] for u in units]
        + [u[1] for u in units],
        smem=1,
    )
    arrived = [moved(out, k, back=True) for k, out in enumerate(outs, 2)]
    mean, level, out = call(
        local_pair,
        "local_pair",
        [((local, width), F32), ((local, HD), F32), message],
        sums,
        [got[0], got[1], root_k, root_t, spread, level_b],
        cost=pl.CostEstimate(
            flops=4 * pair * tokens * width,
            transcendentals=pair * tokens * width // HD,
            bytes_accessed=4 * tokens * wide,
        ),
    )
    arrived.append(moved(out, 1, back=True))
    vmem = pl.BlockSpec(memory_space=pltpu.VMEM)
    return pl.pallas_call(
        join,
        out_shape=jax.ShapeDtypeStruct((local, width), BF16),
        in_specs=[vmem] * (1 + count),
        out_specs=vmem,
        compiler_params=pltpu.CompilerParams(vmem_limit_bytes=8 * 2**20),
        name="join",
    )(*map(near, [*arrived, mean, level]))


def solution(mesh):
    placed = (
        P(("groups", "branch"), "head"),
        P(("groups", "branch"), "head"),
        P(("groups", "branch"), "head"),
        P(("groups", "branch"), None, "head"),
        P(("groups", "branch"), None, "head"),
        P(("groups", "branch")),
        P("groups"),
    )
    return jax.shard_map(
        functools.partial(on_device, "branch", mesh.shape["branch"]),
        mesh=mesh,
        in_specs=placed,
        out_specs=P(("groups", "branch"), "head"),
        check_vma=False,
    )
```

time: 121 us -> 62.2 us (0.51); the launches traced: 119 us -> 61.7 us
  Pallas kernels: 0 us -> 42.4 us
  local copies, waits for them, and re-layouts: 36.7 us -> 0 us
  other arithmetic: 21.3 us -> 0 us
  blocking collectives: 17.6 us -> 0 us
  starting transfers between devices: 0.01 us -> 17.2 us
  matrix products: 15.9 us -> 0 us
  between operations: 14.2 us -> 0.71 us
  waiting for transfers between devices: 12.6 us -> 1.39 us
    pallas_call x0 -> x4, Pallas kernels: none -> 42.4 us  [the longest x3 41.4 us: call(): pl.pallas_call(kernel, out_shape=[pltpu.VMEM(shape, dtype) for shape, dty...]
    dynamic_slice x21 -> x0, local copies, waits for them, and re-layouts: 19.4 us -> none  [the longest x8 11.2 us: on_device(): lax.scan(one_block, empty_part(count, width, head_dim), (root_k, root_v))]
    all_gather x3 -> x0, blocking collectives: 17.6 us -> none  [the longest x2 10.4 us: combined_all(): pieces = jax.tree.map(lambda part: lax.all_gather(part, axis), value)]
    ppermute x0 -> x6, starting transfers between devices: none -> 17.2 us  [moved(): return lax.ppermute(x, axis, [(b, a) for a, b in pairs] if back else pairs)]
    dot_general x35 -> x0, matrix products: 15.9 us -> none  [the longest x16 7.25 us: attend_block(): jnp.einsum('rgpb,bgh->rgph', weights.astype(jnp.bfloat16), values, prefer...]
    all_gather x1 -> x0, waiting for transfers between devices: 12.6 us -> none  [combined_all(): pieces = jax.tree.map(lambda part: lax.all_gather(part, axis), value)]
    add x38 -> x0, other arithmetic: 8.3 us -> none  [the longest x19 8.01 us: combine(): first[2] * scale_a[..., None] + second[2] * scale_b[..., None]]
    unnamed x12 -> x0, local copies, waits for them, and re-layouts: 7.84 us -> none
  transfers between devices with their start and end apart: 1 -> 6, of which waited for: 1 -> 2; matrix products, arithmetic and copies ran while one was open for 0% -> 0% of each run, Pallas kernels for 0% -> 33%
where the time goes in v2:
time: 62.2 us; the launch traced here: 61.7 us
  Pallas kernels  42.4 us (68%)
  starting transfers between devices  17.2 us (28%)
  waiting for transfers between devices  1.39 us (2%)
  between operations  0.71 us (1%)
    pallas_call x3, Pallas kernels, call(): pl.pallas_call(kernel, out_shape=[pltpu.VMEM(shape, dtype) for shape, dty...  41.4 us
    ppermute x6, starting transfers between devices, moved(): return lax.ppermute(x, axis, [(b, a) for a, b in pairs] if back else pairs)  17.2 us
    ppermute x6, waiting for transfers between devices, moved(): return lax.ppermute(x, axis, [(b, a) for a, b in pairs] if back else pairs)  1.39 us
  transfers between devices with their start and end apart: 6, of which 2 were waited for; matrix products, arithmetic and copies ran while one was open for 0% of the time, Pallas kernels for 33%

profile of v2, /device:TPU:0, one launch (start us, length us, event | category | flops | bytes accessed | tf_op | source)
XLA Modules:
  0.0 61.7 jit_solution(5954901406652992861)
XLA Ops:
  0.0 0.5 collective-permute-start
  0.5 2.6 %collective-permute-start.2 = (bf16[16,2048]{1,0:T(8,128)(2,1)}, bf16[16,2048]{1,0:T(8,128)(2,1)S(1)}, u32[]{:S(2)}, u32[]{:S(2)}) collective-permute-start(bf16[16,2048]{1,0:T(8,128)(2,1)} %query_hbm.1), channel_id=1, source_target_pairs={{12,0},{8,4},{4,8},{0,12},{13,1},{9,5},{5,9},{1,13},{14,2},{10,6},... | collective-permute-start | bytes 196616 | tf_op jit(solution)/shard_map/ppermute | solution.py:354
  3.1 0.0 collective-permute-start.1
  3.7 3.6 %prepare.1 = (bf16[4096,256]{1,0:T(8,128)(2,1)S(1)}, bf16[272,4096]{1,0:T(8,128)(2,1)S(1)}, bf16[4096,256]{1,0:T(8,128)(2,1)S(1)}, bf16[272,4096]{1,0:T(8,128)(2...) custom-call(s32[1]{0:T(128)S(6)} %copy.8.length_ref.refs_0_, s32[64]{0:T(128)} %owner_hbm.1, ...), custom_call_target="tpu_custom_call" | custom-call | tf_op jit(solution)/shard_map/prepare/pallas_call | solution.py:319
  7.4 0.0 collective-permute-done.refs_7_.second
  7.4 0.0 collective-permute-done.2.refs_9_
  7.4 0.2 collective-permute-done.1.refs_8_
  7.6 20.9 %main.1 = (bf16[16,2176]{1,0:T(8,128)(2,1)S(1)}, bf16[16,2176]{1,0:T(8,128)(2,1)S(1)}, f32[32,2048]{1,0:T(8,128)S(1)}, f32[32,128]{1,0:T(8,128)S(1)}) custom-call(s32[1]{0:T(128)S(6)} %copy.8.length_ref.refs_0_, bf16[32,64]{1,0:T(8,128)(2,1)S(1)} %get-tuple-element.18.refs_1_, bf16[4096,256]{1,0:T(8,128)(2,1)S(1)} %get-tuple-element.19.refs_2_.root_k, ...), custom_call_target="tpu_custom_call" | custom-call | tf_op jit(solution)/shard_map/main/pallas_call | solution.py:319
  28.5 11.2 %collective-permute-start.3 = (bf16[16,2176]{1,0:T(8,128)(2,1)S(1)}, bf16[16,2176]{1,0:T(8,128)(2,1)S(1)}, u32[]{:S(2)}, u32[]{:S(2)}) collective-permute-start(bf16[16,2176]{1,0:T(8,128)(2,1)S(1)} %get-tuple-element.24), channel_id=1, source_target_pairs={{0,8},{4,12},{8,0},{12,4},{1,9},{5,13},{9,1},{13,5},{2,10},{6,14},... | collective-permute-start | bytes 208904 | tf_op jit(solution)/shard_map/ppermute | solution.py:354
  39.6 2.9 %collective-permute-start.4 = (bf16[16,2176]{1,0:T(8,128)(2,1)S(1)}, bf16[16,2176]{1,0:T(8,128)(2,1)S(1)}, u32[]{:S(2)}, u32[]{:S(2)}) collective-permute-start(bf16[16,2176]{1,0:T(8,128)(2,1)S(1)} %get-tuple-element.25), channel_id=1, source_target_pairs={{0,12},{4,8},{8,4},{12,0},{1,13},{5,9},{9,5},{13,1},{2,14},{6,10},... | collective-permute-start | bytes 208904 | tf_op jit(solution)/shard_map/ppermute | solution.py:354
  42.6 16.9 %local_pair.1 = (f32[16,2048]{1,0:T(8,128)S(1)}, f32[16,128]{1,0:T(8,128)S(1)}, bf16[16,2176]{1,0:T(8,128)(2,1)S(1)}) custom-call(bf16[16,2048]{1,0:T(8,128)(2,1)S(1)} %get-tuple-element.23.refs_6_.first, bf16[16,2048]{1,0:T(8,128)(2,1)S(1)} %collective-permute-done.refs_7_.second, bf16[4096,256]{1,0:T(8,128)(2,1)S(1)} %get-tuple-element.19.refs_2_.root_k, ...), custom_call_target="tpu_custom_call" | custom-call | flops 1073741824 | bytes 4194304 | tf_op jit(solution)/shard_map/local_pair/pallas_call | solution.py:319
  59.4 0.1 collective-permute-start.5
  59.5 0.0 collective-permute-done.3.refs_0_
  59.5 0.0 collective-permute-done.4.refs_1_
  59.5 1.2 %collective-permute-done.5.refs_2_ = bf16[16,2176]{1,0:T(8,128)(2,1)S(1)} collective-permute-done((bf16[16,2176]{1,0:T(8,128)(2,1)S(1)}, bf16[16,2176]{1,0:T(8,128)(2,1)S(1)}, u32[]{:S(2)}, u32[]{:S(2)}) %collective-permute-start.5) | collective-permute-done | bytes 69664 | tf_op jit(solution)/shard_map/ppermute | solution.py:354
  60.8 1.0 %join.1 = bf16[16,2048]{1,0:T(8,128)(2,1)} custom-call(bf16[16,2176]{1,0:T(8,128)(2,1)S(1)} %collective-permute-done.3.refs_0_, bf16[16,2176]{1,0:T(8,128)(2,1)S(1)} %collective-permute-done.4.refs_1_, bf16[16,2176]{1,0:T(8,128)(2,1)S(1)} %collective-permute-done.5.refs_2_, f32[16,2048]{1,0:T(8,128)S(1)} %get-tuple-element.29.refs_3_, ...), custom_call_target="tpu_custom_call" | custom-call | tf_op jit(solution)/shard_map/join/pallas_call | solution.py:417
Async XLA Ops:
  0.0 7.4 %collective-permute-start = (bf16[16,2048]{1,0:T(8,128)(2,1)}, bf16[16,2048]{1,0:T(8,128)(2,1)S(1)}, u32[]{:S(2)}, u32[]{:S(2)}) collective-permute-start(bf16[16,2048]{1,0:T(8,128)(2,1)} %query_hbm.1), channel_id=1, source_target_pairs={{4,0},{0,4},{12,8},{8,12},{5,1},{1,5},{13,9},{9,13},{6,2},{2,6},{1... | collective-permute-start | bytes 196616 | tf_op jit(solution)/shard_map/ppermute | solution.py:354
  0.5 6.9 %collective-permute-start.2 = (bf16[16,2048]{1,0:T(8,128)(2,1)}, bf16[16,2048]{1,0:T(8,128)(2,1)S(1)}, u32[]{:S(2)}, u32[]{:S(2)}) collective-permute-start(bf16[16,2048]{1,0:T(8,128)(2,1)} %query_hbm.1), channel_id=1, source_target_pairs={{12,0},{8,4},{4,8},{0,12},{13,1},{9,5},{5,9},{1,13},{14,2},{10,6},... | collective-permute-start | bytes 196616 | tf_op jit(solution)/shard_map/ppermute | solution.py:354
  3.1 4.5 %collective-permute-start.1 = (bf16[16,2048]{1,0:T(8,128)(2,1)}, bf16[16,2048]{1,0:T(8,128)(2,1)S(1)}, u32[]{:S(2)}, u32[]{:S(2)}) collective-permute-start(bf16[16,2048]{1,0:T(8,128)(2,1)} %query_hbm.1), channel_id=1, source_target_pairs={{8,0},{12,4},{0,8},{4,12},{9,1},{13,5},{1,9},{5,13},{10,2},{14,6},... | collective-permute-start | bytes 196616 | tf_op jit(solution)/shard_map/ppermute | solution.py:354
  28.5 31.0 %collective-permute-start.3 = (bf16[16,2176]{1,0:T(8,128)(2,1)S(1)}, bf16[16,2176]{1,0:T(8,128)(2,1)S(1)}, u32[]{:S(2)}, u32[]{:S(2)}) collective-permute-start(bf16[16,2176]{1,0:T(8,128)(2,1)S(1)} %get-tuple-element.24), channel_id=1, source_target_pairs={{0,8},{4,12},{8,0},{12,4},{1,9},{5,13},{9,1},{13,5},{2,10},{6,14},... | collective-permute-start | bytes 208904 | tf_op jit(solution)/shard_map/ppermute | solution.py:354
  39.6 19.9 %collective-permute-start.4 = (bf16[16,2176]{1,0:T(8,128)(2,1)S(1)}, bf16[16,2176]{1,0:T(8,128)(2,1)S(1)}, u32[]{:S(2)}, u32[]{:S(2)}) collective-permute-start(bf16[16,2176]{1,0:T(8,128)(2,1)S(1)} %get-tuple-element.25), channel_id=1, source_target_pairs={{0,12},{4,8},{8,4},{12,0},{1,13},{5,9},{9,5},{13,1},{2,14},{6,10},... | collective-permute-start | bytes 208904 | tf_op jit(solution)/shard_map/ppermute | solution.py:354
  59.4 1.3 %collective-permute-start.5 = (bf16[16,2176]{1,0:T(8,128)(2,1)S(1)}, bf16[16,2176]{1,0:T(8,128)(2,1)S(1)}, u32[]{:S(2)}, u32[]{:S(2)}) collective-permute-start(bf16[16,2176]{1,0:T(8,128)(2,1)S(1)} %get-tuple-element.28), channel_id=1, source_target_pairs={{0,4},{4,0},{8,12},{12,8},{1,5},{5,1},{9,13},{13,9},{2,6},{6,2},{1... | collective-permute-start | bytes 208904 | tf_op jit(solution)/shard_map/ppermute | solution.py:354

commit v3 on v2

--- a/solution.py
+++ b/solution.py
@@ -40,10 +40,8 @@
     return high, mid, (rest - mid.astype(F32)).astype(BF16)
 
 
-def source_of(me, step, count):
-    if count & (count - 1) == 0:
-        return me ^ step
-    return (me + step) % count
+def source_of(me, step):
+    return me ^ step
 
 
 def stacked(query, group):
@@ -78,22 +76,15 @@
     return [slice(i, i + size) for i in range(0, tokens, size)]
 
 
-def attend(query, keys_ref, turned_ref, acc, marks, length=None):
-    groups = acc.shape[0]
-    queries = [stacked(query, g) for g in range(groups)]
-    whole = blocks(keys_ref.shape[0])
-    first = whole[:1] if length is not None else whole
-    for g, q in enumerate(queries):
+def attend(query, keys_ref, turned_ref, acc, marks):
+    for g in range(acc.shape[0]):
+        q = stacked(query, g)
         mark = jnp.max(dot_nt(keys_ref[:FEW, g * HD : (g + 1) * HD], q), 0, keepdims=True)
         marks[g] = mark
-        parts = [weighted(keys_ref, turned_ref, g, there, q, mark) for there in first]
+        parts = [
+            weighted(keys_ref, turned_ref, g, there, q, mark) for there in blocks(keys_ref.shape[0])
+        ]
         acc[g] = functools.reduce(jnp.add, parts)
-    for there in whole[len(first) :]:
-
-        @pl.when(length > there.start)
-        def _():
-            for g, q in enumerate(queries):
-                acc[g] += weighted(keys_ref, turned_ref, g, there, q, marks[g])
 
 
 def overflowed(acc):
@@ -136,6 +127,12 @@
     return tiles, jnp.concatenate(lines, 0).T
 
 
+def keep(result, mean_ref, level_ref):
+    for head, mean in enumerate(result[0]):
+        mean_ref[:, head * HD : (head + 1) * HD] = mean
+    level_ref[...] = result[1]
+
+
 def joined(tiles, level, spread, level_b):
     top = jnp.maximum(level, level_b)
     weight = jnp.exp2(level - top)
@@ -184,7 +181,7 @@
     me = lax.axis_index(axis)
     row = lax.broadcasted_iota(jnp.int32, (rows, rows), 0)
     column = lax.broadcasted_iota(jnp.int32, (rows, rows), 1)
-    moved = source_of(me, column // local, count) * local + column % local == row
+    moved = source_of(me, column // local) * local + column % local == row
     small[0].wait()
     owner = owner_ref[...].reshape(1, rows).astype(F32)
     owner = dot_nn(jnp.broadcast_to(owner, (8, rows)).astype(BF16), moved.astype(F32).astype(BF16))
@@ -218,10 +215,7 @@
     def _():
         again(query, root_k, root_t, acc, marks, root_k.shape[0])
 
-    tiles, level = finish(acc, marks)
-    for head, mean in enumerate(tiles):
-        mean_ref[:, head * HD : (head + 1) * HD] = mean
-    level_ref[...] = level
+    keep(finish(acc, marks), mean_ref, level_ref)
 
 
 def main(count, *refs):
@@ -232,7 +226,9 @@
     means, refs = refs[:more], refs[more:]
     levels, refs = refs[:more], refs[more:]
     outs, refs = refs[: count - 2], refs[count - 2 :]
-    spread_ref, level_ref, root_acc, root_marks, branch_acc, branch_marks = refs
+    spread_ref, level_ref, root_acc, root_marks, branch_acc, branch_marks, mean_ref, mean_level = refs
+    means = [mean_ref, *means]
+    levels = [mean_level, *levels]
     local = queries[0].shape[0]
     length = length_ref[0]
     picker = picker_ref[...]
@@ -240,11 +236,13 @@
     query = jnp.concatenate(pieces[2:4], 0)
     chosen = dot_nn(picker, jnp.concatenate(pieces, 0)).astype(BF16)
     attend(query, root_k, root_t, root_acc, root_marks)
-    attend(chosen, branch_k, branch_t, branch_acc, branch_marks, length)
+    keep(finish(root_acc, root_marks), mean_ref, mean_level)
+    attend(chosen, branch_k, branch_t, branch_acc, branch_marks)
 
     @pl.when(overflowed(root_acc) | overflowed(branch_acc))
     def _():
         again(query, root_k, root_t, root_acc, root_marks, root_k.shape[0])
+        keep(finish(root_acc, root_marks), mean_ref, mean_level)
         again(chosen, branch_k, branch_t, branch_acc, branch_marks, length)
 
     tiles, level = finish(branch_acc, branch_marks)
@@ -259,12 +257,9 @@
     spread_ref[...] = spread[: 2 * local]
     level_ref[...] = level_b[: 2 * local]
     for pair in range(1, count // 2):
-        if pair == 1:
-            tiles, level = finish(root_acc, root_marks)
-        else:
-            mean = means[pair - 2][...]
-            tiles = [mean[:, i : i + HD] for i in range(0, mean.shape[1], HD)]
-            level = levels[pair - 2][...]
+        mean = means[pair - 1]
+        tiles = [mean[:, i : i + HD] for i in range(0, mean.shape[1], HD)]
+        level = levels[pair - 1][...]
         there = slice(2 * pair * local, 2 * (pair + 1) * local)
         tiles, level = joined(tiles, level, spread[there], level_b[there])
         for j in range(2):
@@ -349,9 +344,8 @@
     message = ((local, width + HD), BF16)
     pair_form = [((pair, width), F32), ((pair, HD), F32)]
 
-    def moved(x, step, back=False):
-        pairs = [(source_of(i, step, count), i) for i in range(count)]
-        return lax.ppermute(x, axis, [(b, a) for a, b in pairs] if back else pairs)
+    def moved(x, step):
+        return lax.ppermute(x, axis, [(source_of(i, step), i) for i in range(count)])
 
     got = {k: moved(queries, k) for k in [*range(2, count), 1]}
     root_k, root_t, branch_k, branch_t, own, picker = call(
@@ -392,14 +386,14 @@
         functools.partial(main, count),
         "main",
         [message] * (count - 2) + pair_form,
-        sums + sums,
+        sums + sums + [pltpu.VMEM(*shape) for shape in pair_form],
         [branch_lengths, picker, root_k, root_t, branch_k, branch_t]
         + [got[k] for k in range(count)]
         + [u[0] for u in units]
         + [u[1] for u in units],
         smem=1,
     )
-    arrived = [moved(out, k, back=True) for k, out in enumerate(outs, 2)]
+    arrived = [moved(out, k) for k, out in enumerate(outs, 2)]
     mean, level, out = call(
         local_pair,
         "local_pair",
@@ -412,7 +406,7 @@
             bytes_accessed=4 * tokens * wide,
         ),
     )
-    arrived.append(moved(out, 1, back=True))
+    arrived.append(moved(out, 1))
     vmem = pl.BlockSpec(memory_space=pltpu.VMEM)
     return pl.pallas_call(
         join,

time: 62.2 us -> 62 us (level)
  Pallas kernels: 42.4 us -> 49.5 us
  starting transfers between devices: 17.2 us -> 10.4 us
    pallas_call x3, Pallas kernels: 41.4 us -> 48.6 us  [call(): pl.pallas_call(kernel, out_shape=[pltpu.VMEM(shape, dtype) for shape, dty...]
    ppermute x6, starting transfers between devices: 17.2 us -> 10.4 us  [moved(): lax.ppermute(x, axis, [(source_of(i, step), i) for i in range(count)])]
where the time goes in v3:
time: 62 us; the launch traced here: 61.9 us
  Pallas kernels  49.5 us (80%)
  starting transfers between devices  10.4 us (17%)
  waiting for transfers between devices  1.23 us (2%)
  between operations  0.69 us (1%)
    pallas_call x3, Pallas kernels, call(): pl.pallas_call(kernel, out_shape=[pltpu.VMEM(shape, dtype) for shape, dty...  48.6 us
    ppermute x6, starting transfers between devices, moved(): lax.ppermute(x, axis, [(source_of(i, step), i) for i in range(count)])  10.4 us
  transfers between devices with their start and end apart: 6, of which 2 were waited for; matrix products, arithmetic and copies ran while one was open for 0% of the time, Pallas kernels for 33%

profile of v3, /device:TPU:0, one launch (start us, length us, event | category | flops | bytes accessed | tf_op | source)
XLA Modules:
  0.0 61.9 jit_solution(13665405881430113916)
XLA Ops:
  0.0 0.5 collective-permute-start
  0.5 2.6 %collective-permute-start.2 = (bf16[16,2048]{1,0:T(8,128)(2,1)}, bf16[16,2048]{1,0:T(8,128)(2,1)S(1)}, u32[]{:S(2)}, u32[]{:S(2)}) collective-permute-start(bf16[16,2048]{1,0:T(8,128)(2,1)} %query_hbm.1), channel_id=1, source_target_pairs={{12,0},{8,4},{4,8},{0,12},{13,1},{9,5},{5,9},{1,13},{14,2},{10,6},... | collective-permute-start | bytes 196616 | tf_op jit(solution)/shard_map/ppermute | solution.py:348
  3.1 0.0 collective-permute-start.1
  3.7 3.6 %prepare.1 = (bf16[4096,256]{1,0:T(8,128)(2,1)S(1)}, bf16[272,4096]{1,0:T(8,128)(2,1)S(1)}, bf16[4096,256]{1,0:T(8,128)(2,1)S(1)}, bf16[272,4096]{1,0:T(8,128)(2...) custom-call(s32[1]{0:T(128)S(6)} %copy.8.length_ref.refs_0_, s32[64]{0:T(128)} %owner_hbm.1, ...), custom_call_target="tpu_custom_call" | custom-call | tf_op jit(solution)/shard_map/prepare/pallas_call | solution.py:314
  7.4 0.0 collective-permute-done.refs_7_.second
  7.4 0.0 collective-permute-done.2.refs_9_
  7.4 0.2 collective-permute-done.1.refs_8_
  7.6 28.1 %main.1 = (bf16[16,2176]{1,0:T(8,128)(2,1)S(1)}, bf16[16,2176]{1,0:T(8,128)(2,1)S(1)}, f32[32,2048]{1,0:T(8,128)S(1)}, f32[32,128]{1,0:T(8,128)S(1)}) custom-call(s32[1]{0:T(128)S(6)} %copy.8.length_ref.refs_0_, bf16[32,64]{1,0:T(8,128)(2,1)S(1)} %get-tuple-element.18.refs_1_, bf16[4096,256]{1,0:T(8,128)(2,1)S(1)} %get-tuple-element.19.refs_2_.root_k, ...), custom_call_target="tpu_custom_call" | custom-call | tf_op jit(solution)/shard_map/main/pallas_call | solution.py:314
  35.6 7.1 %collective-permute-start.3 = (bf16[16,2176]{1,0:T(8,128)(2,1)S(1)}, bf16[16,2176]{1,0:T(8,128)(2,1)S(1)}, u32[]{:S(2)}, u32[]{:S(2)}) collective-permute-start(bf16[16,2176]{1,0:T(8,128)(2,1)S(1)} %get-tuple-element.24), channel_id=1, source_target_pairs={{8,0},{12,4},{0,8},{4,12},{9,1},{13,5},{1,9},{5,13},{10,2},{14,6},... | collective-permute-start | bytes 208904 | tf_op jit(solution)/shard_map/ppermute | solution.py:348
  42.7 0.0 collective-permute-start.4
  42.7 16.9 %local_pair.1 = (f32[16,2048]{1,0:T(8,128)S(1)}, f32[16,128]{1,0:T(8,128)S(1)}, bf16[16,2176]{1,0:T(8,128)(2,1)S(1)}) custom-call(bf16[16,2048]{1,0:T(8,128)(2,1)S(1)} %get-tuple-element.23.refs_6_.first, bf16[16,2048]{1,0:T(8,128)(2,1)S(1)} %collective-permute-done.refs_7_.second, bf16[4096,256]{1,0:T(8,128)(2,1)S(1)} %get-tuple-element.19.refs_2_.root_k, ...), custom_call_target="tpu_custom_call" | custom-call | flops 1073741824 | bytes 4194304 | tf_op jit(solution)/shard_map/local_pair/pallas_call | solution.py:314
  59.6 0.3 collective-permute-start.5
  59.9 0.0 collective-permute-done.3.refs_0_
  59.9 0.0 collective-permute-done.4.refs_1_
  59.9 1.1 %collective-permute-done.5.refs_2_ = bf16[16,2176]{1,0:T(8,128)(2,1)S(1)} collective-permute-done((bf16[16,2176]{1,0:T(8,128)(2,1)S(1)}, bf16[16,2176]{1,0:T(8,128)(2,1)S(1)}, u32[]{:S(2)}, u32[]{:S(2)}) %collective-permute-start.5) | collective-permute-done | bytes 69664 | tf_op jit(solution)/shard_map/ppermute | solution.py:348
  60.9 1.0 %join.1 = bf16[16,2048]{1,0:T(8,128)(2,1)} custom-call(bf16[16,2176]{1,0:T(8,128)(2,1)S(1)} %collective-permute-done.3.refs_0_, bf16[16,2176]{1,0:T(8,128)(2,1)S(1)} %collective-permute-done.4.refs_1_, bf16[16,2176]{1,0:T(8,128)(2,1)S(1)} %collective-permute-done.5.refs_2_, f32[16,2048]{1,0:T(8,128)S(1)} %get-tuple-element.29.refs_3_, ...), custom_call_target="tpu_custom_call" | custom-call | tf_op jit(solution)/shard_map/join/pallas_call | solution.py:411
Async XLA Ops:
  0.0 7.4 %collective-permute-start = (bf16[16,2048]{1,0:T(8,128)(2,1)}, bf16[16,2048]{1,0:T(8,128)(2,1)S(1)}, u32[]{:S(2)}, u32[]{:S(2)}) collective-permute-start(bf16[16,2048]{1,0:T(8,128)(2,1)} %query_hbm.1), channel_id=1, source_target_pairs={{4,0},{0,4},{12,8},{8,12},{5,1},{1,5},{13,9},{9,13},{6,2},{2,6},{1... | collective-permute-start | bytes 196616 | tf_op jit(solution)/shard_map/ppermute | solution.py:348
  0.5 6.9 %collective-permute-start.2 = (bf16[16,2048]{1,0:T(8,128)(2,1)}, bf16[16,2048]{1,0:T(8,128)(2,1)S(1)}, u32[]{:S(2)}, u32[]{:S(2)}) collective-permute-start(bf16[16,2048]{1,0:T(8,128)(2,1)} %query_hbm.1), channel_id=1, source_target_pairs={{12,0},{8,4},{4,8},{0,12},{13,1},{9,5},{5,9},{1,13},{14,2},{10,6},... | collective-permute-start | bytes 196616 | tf_op jit(solution)/shard_map/ppermute | solution.py:348
  3.1 4.5 %collective-permute-start.1 = (bf16[16,2048]{1,0:T(8,128)(2,1)}, bf16[16,2048]{1,0:T(8,128)(2,1)S(1)}, u32[]{:S(2)}, u32[]{:S(2)}) collective-permute-start(bf16[16,2048]{1,0:T(8,128)(2,1)} %query_hbm.1), channel_id=1, source_target_pairs={{8,0},{12,4},{0,8},{4,12},{9,1},{13,5},{1,9},{5,13},{10,2},{14,6},... | collective-permute-start | bytes 196616 | tf_op jit(solution)/shard_map/ppermute | solution.py:348
  35.6 24.3 %collective-permute-start.3 = (bf16[16,2176]{1,0:T(8,128)(2,1)S(1)}, bf16[16,2176]{1,0:T(8,128)(2,1)S(1)}, u32[]{:S(2)}, u32[]{:S(2)}) collective-permute-start(bf16[16,2176]{1,0:T(8,128)(2,1)S(1)} %get-tuple-element.24), channel_id=1, source_target_pairs={{8,0},{12,4},{0,8},{4,12},{9,1},{13,5},{1,9},{5,13},{10,2},{14,6},... | collective-permute-start | bytes 208904 | tf_op jit(solution)/shard_map/ppermute | solution.py:348
  42.7 17.2 %collective-permute-start.4 = (bf16[16,2176]{1,0:T(8,128)(2,1)S(1)}, bf16[16,2176]{1,0:T(8,128)(2,1)S(1)}, u32[]{:S(2)}, u32[]{:S(2)}) collective-permute-start(bf16[16,2176]{1,0:T(8,128)(2,1)S(1)} %get-tuple-element.25), channel_id=1, source_target_pairs={{12,0},{8,4},{4,8},{0,12},{13,1},{9,5},{5,9},{1,13},{14,2},{10,6},... | collective-permute-start | bytes 208904 | tf_op jit(solution)/shard_map/ppermute | solution.py:348
  59.6 1.3 %collective-permute-start.5 = (bf16[16,2176]{1,0:T(8,128)(2,1)S(1)}, bf16[16,2176]{1,0:T(8,128)(2,1)S(1)}, u32[]{:S(2)}, u32[]{:S(2)}) collective-permute-start(bf16[16,2176]{1,0:T(8,128)(2,1)S(1)} %get-tuple-element.28), channel_id=1, source_target_pairs={{4,0},{0,4},{12,8},{8,12},{5,1},{1,5},{13,9},{9,13},{6,2},{2,6},{1... | collective-permute-start | bytes 208904 | tf_op jit(solution)/shard_map/ppermute | solution.py:348

commit v4 on v3

--- a/solution.py
+++ b/solution.py
@@ -222,6 +222,7 @@
     length_ref, picker_ref, root_k, root_t, branch_k, branch_t = refs[:6]
     refs = refs[6:]
     queries, refs = refs[:count], refs[count:]
+    queries = (queries[-1], queries[-2], *queries[:-2])
     more = max(0, count // 2 - 2)
     means, refs = refs[:more], refs[more:]
     levels, refs = refs[:more], refs[more:]
@@ -388,7 +389,7 @@
         [message] * (count - 2) + pair_form,
         sums + sums + [pltpu.VMEM(*shape) for shape in pair_form],
         [branch_lengths, picker, root_k, root_t, branch_k, branch_t]
-        + [got[k] for k in range(count)]
+        + [got[k] for k in [*range(2, count), 1, 0]]
         + [u[0] for u in units]
         + [u[1] for u in units],
         smem=1,

time: 62 us -> 61.8 us (level)
  Pallas kernels: 49.5 us -> 54.7 us
  starting transfers between devices: 10.4 us -> 5.34 us
    pallas_call x3, Pallas kernels: 48.6 us -> 53.7 us  [call(): pl.pallas_call(kernel, out_shape=[pltpu.VMEM(shape, dtype) for shape, dty...]
    ppermute x6, starting transfers between devices: 10.4 us -> 5.34 us  [moved(): lax.ppermute(x, axis, [(source_of(i, step), i) for i in range(count)])]
  transfers between devices with their start and end apart: 6 -> 6, of which waited for: 2 -> 1; matrix products, arithmetic and copies ran while one was open for 0% -> 0% of each run, Pallas kernels for 33% -> 33%
where the time goes in v4:
time: 61.8 us; the launch traced here: 61.7 us
  Pallas kernels  54.7 us (89%)
  starting transfers between devices  5.34 us (9%)
  waiting for transfers between devices  0.91 us (1%)
  between operations  0.71 us (1%)
    pallas_call x3, Pallas kernels, call(): pl.pallas_call(kernel, out_shape=[pltpu.VMEM(shape, dtype) for shape, dty...  53.7 us
    ppermute x6, starting transfers between devices, moved(): lax.ppermute(x, axis, [(source_of(i, step), i) for i in range(count)])  5.34 us
  transfers between devices with their start and end apart: 6, of which 1 were waited for; matrix products, arithmetic and copies ran while one was open for 0% of the time, Pallas kernels for 33%

profile of v4, /device:TPU:0, one launch (start us, length us, event | category | flops | bytes accessed | tf_op | source)
XLA Modules:
  0.0 61.7 jit_solution(17624987302787208627)
XLA Ops:
  0.0 3.0 %collective-permute-start = (bf16[16,2048]{1,0:T(8,128)(2,1)}, bf16[16,2048]{1,0:T(8,128)(2,1)S(1)}, u32[]{:S(2)}, u32[]{:S(2)}) collective-permute-start(bf16[16,2048]{1,0:T(8,128)(2,1)} %query_hbm.1), channel_id=1, source_target_pairs={{8,0},{12,4},{0,8},{4,12},{9,1},{13,5},{1,9},{5,13},{10,2},{14,6},... | collective-permute-start | bytes 196616 | tf_op jit(solution)/shard_map/ppermute | solution.py:349
  3.0 0.0 collective-permute-start.2
  3.0 0.1 collective-permute-start.1
  3.7 3.6 %prepare.1 = (bf16[4096,256]{1,0:T(8,128)(2,1)S(1)}, bf16[272,4096]{1,0:T(8,128)(2,1)S(1)}, bf16[4096,256]{1,0:T(8,128)(2,1)S(1)}, bf16[272,4096]{1,0:T(8,128)(2...) custom-call(s32[1]{0:T(128)S(6)} %copy.8.length_ref.refs_0_, s32[64]{0:T(128)} %owner_hbm.1, ...), custom_call_target="tpu_custom_call" | custom-call | tf_op jit(solution)/shard_map/prepare/pallas_call | solution.py:315
  7.4 0.0 collective-permute-done.refs_6_
  7.4 0.0 collective-permute-done.2.refs_8_.second
  7.4 0.0 collective-permute-done.1.refs_7_
  7.4 33.2 %main.1 = (bf16[16,2176]{1,0:T(8,128)(2,1)S(1)}, bf16[16,2176]{1,0:T(8,128)(2,1)S(1)}, f32[32,2048]{1,0:T(8,128)S(1)}, f32[32,128]{1,0:T(8,128)S(1)}) custom-call(s32[1]{0:T(128)S(6)} %copy.8.length_ref.refs_0_, bf16[32,64]{1,0:T(8,128)(2,1)S(1)} %get-tuple-element.18.refs_1_, bf16[4096,256]{1,0:T(8,128)(2,1)S(1)} %get-tuple-element.19.refs_2_.root_k, ...), custom_call_target="tpu_custom_call" | custom-call | tf_op jit(solution)/shard_map/main/pallas_call | solution.py:315
  40.6 0.1 collective-permute-start.3
  40.7 0.1 collective-permute-start.4
  40.8 16.9 %local_pair.1 = (f32[16,2048]{1,0:T(8,128)S(1)}, f32[16,128]{1,0:T(8,128)S(1)}, bf16[16,2176]{1,0:T(8,128)(2,1)S(1)}) custom-call(bf16[16,2048]{1,0:T(8,128)(2,1)S(1)} %get-tuple-element.23.refs_9_.first, bf16[16,2048]{1,0:T(8,128)(2,1)S(1)} %collective-permute-done.2.refs_8_.second, bf16[4096,256]{1,0:T(8,128)(2,1)S(1)} %get-tuple-element.19.refs_2_.root_k, ...), custom_call_target="tpu_custom_call" | custom-call | flops 1073741824 | bytes 4194304 | tf_op jit(solution)/shard_map/local_pair/pallas_call | solution.py:315
  57.7 2.1 %collective-permute-start.5 = (bf16[16,2176]{1,0:T(8,128)(2,1)S(1)}, bf16[16,2176]{1,0:T(8,128)(2,1)S(1)}, u32[]{:S(2)}, u32[]{:S(2)}) collective-permute-start(bf16[16,2176]{1,0:T(8,128)(2,1)S(1)} %get-tuple-element.28), channel_id=1, source_target_pairs={{4,0},{0,4},{12,8},{8,12},{5,1},{1,5},{13,9},{9,13},{6,2},{2,6},{1... | collective-permute-start | bytes 208904 | tf_op jit(solution)/shard_map/ppermute | solution.py:349
  59.8 0.0 collective-permute-done.3.refs_0_
  59.8 0.0 collective-permute-done.4.refs_1_
  59.8 0.9 %collective-permute-done.5.refs_2_ = bf16[16,2176]{1,0:T(8,128)(2,1)S(1)} collective-permute-done((bf16[16,2176]{1,0:T(8,128)(2,1)S(1)}, bf16[16,2176]{1,0:T(8,128)(2,1)S(1)}, u32[]{:S(2)}, u32[]{:S(2)}) %collective-permute-start.5) | collective-permute-done | bytes 69664 | tf_op jit(solution)/shard_map/ppermute | solution.py:349
  60.7 1.0 %join.1 = bf16[16,2048]{1,0:T(8,128)(2,1)} custom-call(bf16[16,2176]{1,0:T(8,128)(2,1)S(1)} %collective-permute-done.3.refs_0_, bf16[16,2176]{1,0:T(8,128)(2,1)S(1)} %collective-permute-done.4.refs_1_, bf16[16,2176]{1,0:T(8,128)(2,1)S(1)} %collective-permute-done.5.refs_2_, f32[16,2048]{1,0:T(8,128)S(1)} %get-tuple-element.29.refs_3_, ...), custom_call_target="tpu_custom_call" | custom-call | tf_op jit(solution)/shard_map/join/pallas_call | solution.py:412
Async XLA Ops:
  0.0 7.4 %collective-permute-start = (bf16[16,2048]{1,0:T(8,128)(2,1)}, bf16[16,2048]{1,0:T(8,128)(2,1)S(1)}, u32[]{:S(2)}, u32[]{:S(2)}) collective-permute-start(bf16[16,2048]{1,0:T(8,128)(2,1)} %query_hbm.1), channel_id=1, source_target_pairs={{8,0},{12,4},{0,8},{4,12},{9,1},{13,5},{1,9},{5,13},{10,2},{14,6},... | collective-permute-start | bytes 196616 | tf_op jit(solution)/shard_map/ppermute | solution.py:349
  3.0 4.4 %collective-permute-start.2 = (bf16[16,2048]{1,0:T(8,128)(2,1)}, bf16[16,2048]{1,0:T(8,128)(2,1)S(1)}, u32[]{:S(2)}, u32[]{:S(2)}) collective-permute-start(bf16[16,2048]{1,0:T(8,128)(2,1)} %query_hbm.1), channel_id=1, source_target_pairs={{4,0},{0,4},{12,8},{8,12},{5,1},{1,5},{13,9},{9,13},{6,2},{2,6},{1... | collective-permute-start | bytes 196616 | tf_op jit(solution)/shard_map/ppermute | solution.py:349
  3.0 4.4 %collective-permute-start.1 = (bf16[16,2048]{1,0:T(8,128)(2,1)}, bf16[16,2048]{1,0:T(8,128)(2,1)S(1)}, u32[]{:S(2)}, u32[]{:S(2)}) collective-permute-start(bf16[16,2048]{1,0:T(8,128)(2,1)} %query_hbm.1), channel_id=1, source_target_pairs={{12,0},{8,4},{4,8},{0,12},{13,1},{9,5},{5,9},{1,13},{14,2},{10,6},... | collective-permute-start | bytes 196616 | tf_op jit(solution)/shard_map/ppermute | solution.py:349
  40.6 19.2 %collective-permute-start.3 = (bf16[16,2176]{1,0:T(8,128)(2,1)S(1)}, bf16[16,2176]{1,0:T(8,128)(2,1)S(1)}, u32[]{:S(2)}, u32[]{:S(2)}) collective-permute-start(bf16[16,2176]{1,0:T(8,128)(2,1)S(1)} %get-tuple-element.24), channel_id=1, source_target_pairs={{8,0},{12,4},{0,8},{4,12},{9,1},{13,5},{1,9},{5,13},{10,2},{14,6},... | collective-permute-start | bytes 208904 | tf_op jit(solution)/shard_map/ppermute | solution.py:349
  40.7 19.1 %collective-permute-start.4 = (bf16[16,2176]{1,0:T(8,128)(2,1)S(1)}, bf16[16,2176]{1,0:T(8,128)(2,1)S(1)}, u32[]{:S(2)}, u32[]{:S(2)}) collective-permute-start(bf16[16,2176]{1,0:T(8,128)(2,1)S(1)} %get-tuple-element.25), channel_id=1, source_target_pairs={{12,0},{8,4},{4,8},{0,12},{13,1},{9,5},{5,9},{1,13},{14,2},{10,6},... | collective-permute-start | bytes 208904 | tf_op jit(solution)/shard_map/ppermute | solution.py:349
  57.7 3.0 %collective-permute-start.5 = (bf16[16,2176]{1,0:T(8,128)(2,1)S(1)}, bf16[16,2176]{1,0:T(8,128)(2,1)S(1)}, u32[]{:S(2)}, u32[]{:S(2)}) collective-permute-start(bf16[16,2176]{1,0:T(8,128)(2,1)S(1)} %get-tuple-element.28), channel_id=1, source_target_pairs={{4,0},{0,4},{12,8},{8,12},{5,1},{1,5},{13,9},{9,13},{6,2},{2,6},{1... | collective-permute-start | bytes 208904 | tf_op jit(solution)/shard_map/ppermute | solution.py:349
